TPU v7x, 256 devices: a whole 4x4x8 slice. The times are simulated.
256 devices in a mesh: trow: 32 (over z, x_lo, core), tcol: 8 (over x_hi, y).
Axes of the slice: x: 4 (x_hi: 2, x_lo: 2; x = x_hi * 2 + x_lo), y: 4, z: 8, core: 2. Of those that a mesh axis runs over, the one named last changes fastest.
Arguments:
- lesser: bfloat16 [2, 3072, 3072], P(None, 'trow', 'tcol'), may hold values from -4 to 4
- greater: bfloat16 [2, 3072, 3072], P(None, 'trow', 'tcol'), may hold values from -4 to 4
- hopping: bfloat16 [32, 32], replicated, may hold values from -1 to 1
- coupling: float32 [32], replicated, may hold values from 0.5 to 1.5
Outputs:
- lesser_out: bfloat16 [2, 3072, 3072], P(None, 'trow', 'tcol')
- greater_out: bfloat16 [2, 3072, 3072], P(None, 'trow', 'tcol')
All inputs are finite; a program needn't handle non-finite values.
Results may differ from a plain program's by a relative error of at most 0.0068.
Values may be sent and summed in bfloat16 or wider, within the bound.
A program may use at most 64 MiB of HBM per device.

v0:
```python
import jax
import jax.numpy as jnp
from jax import lax
from jax.sharding import PartitionSpec as P

ORBITAL_COUNT = 32
STEPS = 2


def spread(block, axis, owner):
    block = jnp.where(lax.axis_index(axis) == owner, block, jnp.zeros_like(block))
    return lax.psum(block, axis)


def entering(part, axis, combine, identity):
    place = lax.axis_index(axis)
    gathered = jax.tree.map(lambda a: lax.all_gather(a, axis), part)
    state = jax.tree.map(lambda a, e: jnp.zeros_like(a) + jnp.asarray(e, a.dtype), part, identity)

    def one(turn, state):
        return combine(
            state, jax.tree.map(lambda a: lax.dynamic_index_in_dim(a, turn, 0, False), gathered)
        )

    return lax.fori_loop(0, place, one, state)


def pair_energy(factor, partner, row_weights, col_weights):
    base_r = factor[0].astype(jnp.float32)
    base_i = factor[1].astype(jnp.float32)
    mirror_r = partner[0].astype(jnp.float32)
    mirror_i = partner[1].astype(jnp.float32)
    square_r = base_r * base_r - base_i * base_i
    square_i = 2.0 * base_r * base_i
    scaling = row_weights[:, None] * col_weights[None, :]
    real_part = (square_r * mirror_r - square_i * mirror_i) * scaling
    imag_part = (square_r * mirror_i + square_i * mirror_r) * scaling
    return jnp.stack([real_part, imag_part]).astype(jnp.bfloat16)


def matmul_f32(left_op, right_op):
    return jnp.dot(left_op, right_op, preferred_element_type=jnp.float32)


def complex_product(left_op, right_op):
    real_part = matmul_f32(left_op[0], right_op[0]) - matmul_f32(left_op[1], right_op[1])
    imag_part = matmul_f32(left_op[0], right_op[1]) + matmul_f32(left_op[1], right_op[0])
    return (real_part, imag_part)


def add_pair(earlier, later):
    return jax.tree.map(jnp.add, earlier, later)


def local_derivatives(current_state, collision_real, collision_imaginary, hopping, timeline_rows):
    column_total = current_state.shape[2]
    blocks = current_state.reshape(2, timeline_rows, ORBITAL_COUNT, column_total)
    hopping_applied = jnp.einsum(
        "ik,ctkx->ctix", hopping, blocks, preferred_element_type=jnp.float32
    )
    derivative_real = hopping_applied[1] + collision_imaginary.reshape(
        timeline_rows, ORBITAL_COUNT, column_total
    )
    derivative_imaginary = -(
        hopping_applied[0] + collision_real.reshape(timeline_rows, ORBITAL_COUNT, column_total)
    )
    return jnp.stack([derivative_real, derivative_imaginary])


def renew(rates, carried, boundary_rows, time_increment):
    summed = jnp.cumsum(rates, axis=1)
    before = jnp.concatenate([jnp.zeros_like(rates[:, :1]), summed[:, :-1]], axis=1)
    renewed = boundary_rows.astype(jnp.float32)[:, None] + time_increment * (
        carried[:, None] + before
    )
    return renewed.reshape(2, -1, rates.shape[3]).astype(jnp.bfloat16)


def per_device(lesser, greater, hopping, coupling):
    trow_count = lax.axis_size("trow")
    position = lax.axis_index("trow")
    row_count = lesser.shape[1]
    column_total = lesser.shape[2]
    timeline_rows = row_count // ORBITAL_COUNT
    total_times = row_count * trow_count // ORBITAL_COUNT
    time_increment = 3.0 / total_times
    weights = jnp.tile(coupling, total_times)
    own_weights = lax.dynamic_slice_in_dim(weights, position * row_count, row_count, 0)
    boundary_lesser, boundary_greater = (
        spread(lesser[:, :ORBITAL_COUNT, :], "trow", 0),
        spread(greater[:, :ORBITAL_COUNT, :], "trow", 0),
    )
    current_lesser = lesser
    current_greater = greater
    for sweep in range(STEPS):
        row_l, row_g = (
            lax.all_gather(current_lesser, "tcol", axis=2, tiled=True),
            lax.all_gather(current_greater, "tcol", axis=2, tiled=True),
        )
        col_l, col_g = (
            lax.all_to_all(row_l, "trow", split_axis=2, concat_axis=1, tiled=True),
            lax.all_to_all(row_g, "trow", split_axis=2, concat_axis=1, tiled=True),
        )
        hist_l, hist_g = (
            lax.all_gather(current_lesser, "trow", axis=1, tiled=True),
            lax.all_gather(current_greater, "trow", axis=1, tiled=True),
        )
        sigma_less = pair_energy(row_l, jnp.swapaxes(col_g, 1, 2), own_weights, weights)
        sigma_great = pair_energy(row_g, jnp.swapaxes(col_l, 1, 2), own_weights, weights)
        greater_real, greater_imaginary = complex_product(sigma_great, hist_l)
        lesser_real, lesser_imaginary = complex_product(sigma_less, hist_g)
        collision_real = time_increment * (greater_real - lesser_real)
        collision_imaginary = time_increment * (greater_imaginary - lesser_imaginary)
        derivatives_lesser = local_derivatives(
            current_lesser, collision_real, collision_imaginary, hopping, timeline_rows
        )
        derivatives_greater = local_derivatives(
            current_greater, collision_real, collision_imaginary, hopping, timeline_rows
        )
        zero_block = jnp.zeros((2, ORBITAL_COUNT, column_total), jnp.float32)
        carry_l, carry_g = entering(
            (jnp.sum(derivatives_lesser, axis=1), jnp.sum(derivatives_greater, axis=1)),
            "trow",
            add_pair,
            (zero_block, zero_block),
        )
        current_lesser = renew(derivatives_lesser, carry_l, boundary_lesser, time_increment)
        current_greater = renew(derivatives_greater, carry_g, boundary_greater, time_increment)
    return (current_lesser, current_greater)


def solution(mesh):
    in_specs = (P(None, "trow", "tcol"), P(None, "trow", "tcol"), P(), P())
    out_specs = (P(None, "trow", "tcol"), P(None, "trow", "tcol"))
    return jax.shard_map(
        per_device, mesh=mesh, in_specs=in_specs, out_specs=out_specs, check_vma=False
    )
```

profile of v0, /device:TPU:231, one launch (start us, length us, event | category | flops | bytes accessed | tf_op | source)
XLA Modules:
  0.0 1083.1 jit_solution(3352919387300802793)
XLA Ops:
  10.0 50.4 %all-gather.19.cloned.1.call-done = bf16[2,96,3072]{2,1,0:T(8,128)(2,1)} async-done(((bf16[2,96,384]{2,1,0:T(8,128)(2,1)}), bf16[2,96,3072]{2,1,0:T(8,128)(2,1)}) %all-gather.19.cloned.1.call-update) | async-done | bytes 1179664 | tf_op jit(solution)/shard_map/all_gather | solution.py:97
  60.4 4.5 copy.22
  64.8 8.8 all-to-all-start
  73.6 44.0 %all-gather.17.cloned.1.call-done = bf16[2,96,3072]{2,1,0:T(8,128)(2,1)} async-done(((bf16[2,96,384]{2,1,0:T(8,128)(2,1)}), bf16[2,96,3072]{2,1,0:T(8,128)(2,1)}) %all-gather.17.cloned.1.call-update) | async-done | bytes 1179664 | tf_op jit(solution)/shard_map/all_gather | solution.py:98
  117.7 4.5 copy.24
  122.1 8.4 all-to-all-start.1
  140.3 38.0 %all-to-all-done.1 = bf16[2,96,3072]{1,0,2:T(2,128)(2,1)S(1)} async-done(((bf16[2,96,3072]{1,0,2:T(2,128)(2,1)}), bf16[2,96,3072]{1,0,2:T(2,128)(2,1)S(1)}, u32[]{:S(2)}, u32[]{:S(2)}) %all-to-all-start.1) | async-done | bytes 1179680 | tf_op jit(solution)/shard_map/all_to_all | solution.py:102
  186.7 17.4 %all-gather.23.cloned.1.call-done = bf16[2,3072,384]{2,1,0:T(8,128)(2,1)} async-done(((bf16[2,96,384]{2,1,0:T(8,128)(2,1)}), bf16[2,3072,384]{2,1,0:T(8,128)(2,1)}) %all-gather.23.cloned.1.call-update) | async-done | bytes 4718608 | tf_op jit(solution)/shard_map/all_gather | solution.py:106
  209.8 61.7 %all-gather.21.cloned.1.call-done = bf16[2,3072,384]{2,1,0:T(8,128)(2,1)} async-done(((bf16[2,96,384]{2,1,0:T(8,128)(2,1)}), bf16[2,3072,384]{2,1,0:T(8,128)(2,1)}) %all-gather.21.cloned.1.call-update) | async-done | bytes 4718608 | tf_op jit(solution)/shard_map/all_gather | solution.py:105
  279.3 192.0 %all-reduce.7.cloned.1.call-done = (bf16[2,32,384]{2,1,0:T(8,128)(2,1)}, bf16[2,32,384]{2,1,0:T(8,128)(2,1)}) async-done(((bf16[2,32,384]{2,1,0:T(8,128)(2,1)}, bf16[2,32,384]{2,1,0:T(8,128)(2,1)}), (bf16[2,32,384]{2,1,0:T(8,128)(2,1)}, bf16[2,32,384]{2,1,0:T(8,128)(2,1)})) %all-reduce.7.cloned.1.call-update) | async-done | bytes 98320 | tf_op jit(solution)/shard_map/psum | solution.py:12
  472.2 66.6 %all-gather.35.cloned.1.call-done = f32[64,32,384]{2,1,0:T(8,128)} async-done(((f32[2,32,384]{2,1,0:T(8,128)}), f32[64,32,384]{2,1,0:T(8,128)}) %all-gather.35.cloned.1.call-update) | async-done | bytes 3145744 | tf_op jit(solution)/shard_map/all_gather | solution.py:17
  538.9 68.4 %all-gather.33.cloned.1.call-done = f32[64,32,384]{2,1,0:T(8,128)} async-done(((f32[2,32,384]{2,1,0:T(8,128)}), f32[64,32,384]{2,1,0:T(8,128)}) %all-gather.33.cloned.1.call-update) | async-done | bytes 3145744 | tf_op jit(solution)/shard_map/all_gather | solution.py:17
  607.2 31.9 %while.24 = (s32[]{:T(128)}, f32[2,32,384]{2,1,0:T(8,128)S(1)}, f32[2,32,384]{2,1,0:T(8,128)S(1)}, s32[]{:T(128)}, f32[32,2,32,384]{3,2,1,0:T(8,128)}, /*index=5...) while((s32[]{:T(128)}, f32[2,32,384]{2,1,0:T(8,128)S(1)}, f32[2,32,384]{2,1,0:T(8,128)S(1)}, ...), condition=%wide.region_4.5_spmd, body=%wide.region_3.4_spmd.sunk | while | flops 49157 | bytes 589955 | solution.py:25
  642.1 45.4 %all-gather.27.cloned.1.call-done = bf16[2,96,3072]{2,1,0:T(8,128)(2,1)} async-done(((bf16[2,96,384]{2,1,0:T(8,128)(2,1)}), bf16[2,96,3072]{2,1,0:T(8,128)(2,1)}) %all-gather.27.cloned.1.call-update) | async-done | bytes 1179664 | tf_op jit(solution)/shard_map/all_gather | solution.py:97
  687.5 4.5 copy.26
  692.0 8.8 all-to-all-start.2
  700.8 44.1 %all-gather.25.cloned.1.call-done = bf16[2,96,3072]{2,1,0:T(8,128)(2,1)} async-done(((bf16[2,96,384]{2,1,0:T(8,128)(2,1)}), bf16[2,96,3072]{2,1,0:T(8,128)(2,1)}) %all-gather.25.cloned.1.call-update) | async-done | bytes 1179664 | tf_op jit(solution)/shard_map/all_gather | solution.py:98
  749.3 8.8 all-to-all-start.3
  766.4 39.5 %all-to-all-done.3 = bf16[2,96,3072]{1,0,2:T(2,128)(2,1)S(1)} async-done(((bf16[2,96,3072]{1,0,2:T(2,128)(2,1)}), bf16[2,96,3072]{1,0,2:T(2,128)(2,1)S(1)}, u32[]{:S(2)}, u32[]{:S(2)}) %all-to-all-start.3) | async-done | bytes 1179680 | tf_op jit(solution)/shard_map/all_to_all | solution.py:102
  814.2 17.6 %all-gather.31.cloned.1.call-done = bf16[2,3072,384]{2,1,0:T(8,128)(2,1)} async-done(((bf16[2,96,384]{2,1,0:T(8,128)(2,1)}), bf16[2,3072,384]{2,1,0:T(8,128)(2,1)}) %all-gather.31.cloned.1.call-update) | async-done | bytes 4718608 | tf_op jit(solution)/shard_map/all_gather | solution.py:106
  837.0 63.3 %all-gather.29.cloned.1.call-done = bf16[2,3072,384]{2,1,0:T(8,128)(2,1)} async-done(((bf16[2,96,384]{2,1,0:T(8,128)(2,1)}), bf16[2,3072,384]{2,1,0:T(8,128)(2,1)}) %all-gather.29.cloned.1.call-update) | async-done | bytes 4718608 | tf_op jit(solution)/shard_map/all_gather | solution.py:105
  910.4 65.0 %all-gather.39.cloned.1.call-done = f32[64,32,384]{2,1,0:T(8,128)} async-done(((f32[2,32,384]{2,1,0:T(8,128)}), f32[64,32,384]{2,1,0:T(8,128)}) %all-gather.39.cloned.1.call-update) | async-done | bytes 3145744 | tf_op jit(solution)/shard_map/all_gather | solution.py:17
  975.5 68.4 %all-gather.37.cloned.1.call-done = f32[64,32,384]{2,1,0:T(8,128)} async-done(((f32[2,32,384]{2,1,0:T(8,128)}), f32[64,32,384]{2,1,0:T(8,128)}) %all-gather.37.cloned.1.call-update) | async-done | bytes 3145744 | tf_op jit(solution)/shard_map/all_gather | solution.py:17
  1043.8 31.9 %while.25 = (s32[]{:T(128)}, f32[2,32,384]{2,1,0:T(8,128)S(1)}, f32[2,32,384]{2,1,0:T(8,128)S(1)}, s32[]{:T(128)}, f32[32,2,32,384]{3,2,1,0:T(8,128)}, /*index=5...) while((s32[]{:T(128)}, f32[2,32,384]{2,1,0:T(8,128)S(1)}, f32[2,32,384]{2,1,0:T(8,128)S(1)}, ...), condition=%wide.region_11.12_spmd, body=%wide.region_10.11_spmd.sunk | while | flops 49157 | bytes 589955 | solution.py:25
  (195 shorter events, 137.0 us)
Async XLA Ops:
  7.2 125.0 %copy-start = (bf16[32,32]{1,0:T(8,128)(2,1)S(1)}, bf16[32,32]{1,0:T(8,128)(2,1)}, u32[]{:S(2)}) copy-start(bf16[32,32]{1,0:T(8,128)(2,1)} %param.10) | copy-start | bytes 6148
  7.2 53.2 %all-gather.19.cloned.1.call-start = ((), (), s32[]{:S(2)}) async-start(), calls=%async_computation.5 | async-start | bytes 1327104 | tf_op jit(solution)/shard_map/all_gather | solution.py:97
  7.9 109.8 %all-gather.17.cloned.1.call-start = ((), (), s32[]{:S(2)}) async-start(), calls=%async_computation.4 | async-start | bytes 1327104 | tf_op jit(solution)/shard_map/all_gather | solution.py:98
  8.7 195.5 %all-gather.23.cloned.1.call-start = ((), (), s32[]{:S(2)}) async-start(), calls=%async_computation.7 | async-start | bytes 4866048 | tf_op jit(solution)/shard_map/all_gather | solution.py:106
  9.4 262.2 %all-gather.21.cloned.1.call-start = ((), (), s32[]{:S(2)}) async-start(), calls=%async_computation.6 | async-start | bytes 4866048 | tf_op jit(solution)/shard_map/all_gather | solution.py:105
  64.8 57.3 %all-to-all-start = ((bf16[2,96,3072]{1,0,2:T(2,128)(2,1)}), bf16[2,96,3072]{1,0,2:T(2,128)(2,1)S(1)}, u32[]{:S(2)}, u32[]{:S(2)}) async-start(bf16[2,96,3072]{1,0,2:T(2,128)(2,1)} %copy.22), calls=%async_computation | async-start | bytes 3145728 | tf_op jit(solution)/shard_map/all_to_all | solution.py:101
  122.1 9.8 copy-start.18
  122.1 56.2 %all-to-all-start.1 = ((bf16[2,96,3072]{1,0,2:T(2,128)(2,1)}), bf16[2,96,3072]{1,0,2:T(2,128)(2,1)S(1)}, u32[]{:S(2)}, u32[]{:S(2)}) async-start(bf16[2,96,3072]{1,0,2:T(2,128)(2,1)} %copy.24), calls=%async_computation.1 | async-start | bytes 3145728 | tf_op jit(solution)/shard_map/all_to_all | solution.py:102
  130.5 340.8 %all-reduce.7.cloned.1.call-start = ((), (), s32[]{:S(2)}) async-start(), calls=%async_computation.16 | async-start | bytes 196608 | tf_op jit(solution)/shard_map/psum | solution.py:12
  131.9 407.0 %all-gather.35.cloned.1.call-start = ((), (), s32[]{:S(2)}) async-start(), calls=%async_computation.13 | async-start | bytes 3244032 | tf_op jit(solution)/shard_map/all_gather | solution.py:17
  132.0 50.3 %copy-start.15 = (f32[3072]{0:T(1024)}, f32[3072]{0:T(1024)S(1)}, u32[]{:S(2)}) copy-start(f32[3072]{0:T(1024)S(1)} %tile.10) | copy-start | bytes 36868
  278.5 328.7 %all-gather.33.cloned.1.call-start = ((), (), s32[]{:S(2)}) async-start(), calls=%async_computation.12 | async-start | bytes 3244032 | tf_op jit(solution)/shard_map/all_gather | solution.py:17
  279.3 408.3 %all-gather.27.cloned.1.call-start = ((), (), s32[]{:S(2)}) async-start(), calls=%async_computation.9 | async-start | bytes 1327104 | tf_op jit(solution)/shard_map/all_gather | solution.py:97
  607.2 32.6 %copy-start.17 = (bf16[2,32,384]{2,1,0:T(8,128)(2,1)S(1)}, bf16[2,32,384]{2,1,0:T(8,128)(2,1)}, u32[]{:S(2)}) copy-start(bf16[2,32,384]{2,1,0:T(8,128)(2,1)} %get-tuple-element.98) | copy-start | bytes 147460
  639.8 105.0 %all-gather.25.cloned.1.call-start = ((), (), s32[]{:S(2)}) async-start(), calls=%async_computation.8 | async-start | bytes 1327104 | tf_op jit(solution)/shard_map/all_gather | solution.py:98
  639.9 52.1 %copy-start.11 = (f32[2,32,384]{2,1,0:T(8,128)}, f32[2,32,384]{2,1,0:T(8,128)S(1)}, u32[]{:S(2)}) copy-start(f32[2,32,384]{2,1,0:T(8,128)S(1)} %convert_element_type.128) | copy-start | bytes 294916
  640.8 191.1 %all-gather.31.cloned.1.call-start = ((), (), s32[]{:S(2)}) async-start(), calls=%async_computation.11 | async-start | bytes 4866048 | tf_op jit(solution)/shard_map/all_gather | solution.py:106
  641.4 258.9 %all-gather.29.cloned.1.call-start = ((), (), s32[]{:S(2)}) async-start(), calls=%async_computation.10 | async-start | bytes 4866048 | tf_op jit(solution)/shard_map/all_gather | solution.py:105
  692.0 57.3 %all-to-all-start.2 = ((bf16[2,96,3072]{1,0,2:T(2,128)(2,1)}), bf16[2,96,3072]{1,0,2:T(2,128)(2,1)S(1)}, u32[]{:S(2)}, u32[]{:S(2)}) async-start(bf16[2,96,3072]{1,0,2:T(2,128)(2,1)} %copy.26), calls=%async_computation.2 | async-start | bytes 3145728 | tf_op jit(solution)/shard_map/all_to_all | solution.py:101
  749.3 9.7 copy-start.4
  749.3 56.5 %all-to-all-start.3 = ((bf16[2,96,3072]{1,0,2:T(2,128)(2,1)}), bf16[2,96,3072]{1,0,2:T(2,128)(2,1)S(1)}, u32[]{:S(2)}, u32[]{:S(2)}) async-start(bf16[2,96,3072]{1,0,2:T(2,128)(2,1)} %copy.28), calls=%async_computation.3 | async-start | bytes 3145728 | tf_op jit(solution)/shard_map/all_to_all | solution.py:102
  758.1 217.3 %all-gather.39.cloned.1.call-start = ((), (), s32[]{:S(2)}) async-start(), calls=%async_computation.15 | async-start | bytes 3244032 | tf_op jit(solution)/shard_map/all_gather | solution.py:17
  909.4 134.4 %all-gather.37.cloned.1.call-start = ((), (), s32[]{:S(2)}) async-start(), calls=%async_computation.14 | async-start | bytes 3244032 | tf_op jit(solution)/shard_map/all_gather | solution.py:17
  1043.8 31.9 %copy-start.12 = (f32[2,32,384]{2,1,0:T(8,128)S(1)}, f32[2,32,384]{2,1,0:T(8,128)}, u32[]{:S(2)}) copy-start(f32[2,32,384]{2,1,0:T(8,128)} %copy-done.11) | copy-start | bytes 294916
  (16 other events, 62.7 us)
Sparse Core Ops, SparseCore 0:
  10.5 49.8 all-gather.18
  62.8 54.7 all-gather.16
  119.5 84.6 all-gather.22
  205.8 65.7 all-gather.20
  274.1 197.2 all-reduce.6
  473.8 65.0 all-gather.34
  541.4 65.7 all-gather.32
  640.0 47.5 all-gather.26
  690.9 53.9 all-gather.24
  747.2 84.5 all-gather.30
  834.3 65.8 all-gather.28
  909.6 65.8 all-gather.38
  978.0 65.7 all-gather.36
where the time goes:
time: 1090 us; the launch traced here: 1080 us
  waiting for transfers between devices  886 us (81%)
  other arithmetic  78.1 us (7%)
  local copies, waits for them, and re-layouts  40 us (4%)
  starting transfers between devices  35.3 us (3%)
  matrix products  27.8 us (3%)
  between operations  14.4 us (1%)
    all_gather x4, waiting for transfers between devices, entering(): gathered = jax.tree.map(lambda a: lax.all_gather(a, axis), part)  268 us
    psum x1, waiting for transfers between devices, spread(): return lax.psum(block, axis)  192 us
    all_gather x2, waiting for transfers between devices, per_device(): lax.all_gather(current_lesser, 'trow', axis=1, tiled=True)  125 us
    all_gather x2, waiting for transfers between devices, per_device(): lax.all_gather(current_lesser, 'tcol', axis=2, tiled=True)  95.8 us
    all_gather x2, waiting for transfers between devices, per_device(): lax.all_gather(current_greater, 'tcol', axis=2, tiled=True)  88.1 us
    all_to_all x2, waiting for transfers between devices, per_device(): lax.all_to_all(row_g, 'trow', split_axis=2, concat_axis=1, tiled=True)  77.5 us
    add x62, other arithmetic, add_pair(): return jax.tree.map(jnp.add, earlier, later)  62.1 us
    all_gather x2, waiting for transfers between devices, per_device(): lax.all_gather(current_greater, 'trow', axis=1, tiled=True)  35 us
  transfers between devices with their start and end apart: 17, of which 15 were waited for; matrix products, arithmetic and copies ran while one was open for 5% of the time, Pallas kernels for 0%

commit v1 on v0

v1 whole, which is shorter than its diff:
```python
import functools

import jax
import jax.numpy as jnp
from jax import lax
from jax.experimental import pallas as pl
from jax.experimental.pallas import tpu as pltpu
from jax.sharding import PartitionSpec as P

MESH = pl.DeviceIdType.MESH
ORB = 32
STEPS = 2
N = 8
Q = 4
Y = 4
F32 = jnp.float32
BF16 = jnp.bfloat16
NT = (((1,), (1,)), ((), ()))
NN = (((1,), (0,)), ((), ()))


def dot(a, b, dims=NN):
    return lax.dot_general(a, b, dims, preferred_element_type=F32)


def kernel(
    dt, x, w, h3, out,
    xq, t1, t2, f, sg, hb, acc, bm, rs_s, rs_r, zt_s, zt_r, ax_s, ax_r, ed_r, a_s, a_r,
    s_t1, r_t1, s_t2, r_t2, s_t3, r_t3, s_q, r_q, s_h, r_h, s_s, r_s,
    s_rs, r_rs, s_zt, r_zt, s_ax, r_ax, s_ed, r_ed, s_a, r_a,
):
    rows = x.shape[1]
    cols = x.shape[2]
    times = rows // ORB
    half = rows // 2
    r = lax.axis_index("trow")
    b = lax.axis_index("tcol")
    z, q = r // Q, r % Q
    xh, y = b // Y, b % Y

    def at_z(zz):
        return {"trow": zz * Q + q, "tcol": b}

    def at_q(qq):
        return {"trow": z * Q + qq, "tcol": b}

    def at_b(bb):
        return {"trow": r, "tcol": bb}

    started = []

    def send(src, dst, ss, rs, where):
        copy = pltpu.make_async_remote_copy(
            src_ref=src, dst_ref=dst, send_sem=ss, recv_sem=rs, device_id=where, device_id_type=MESH
        )
        copy.start()
        return copy

    def push(src, dst, ss, rs, where):
        started.append(send(src, dst, ss, rs, where))

    def arrive(dst, ss, rs):
        pltpu.make_async_remote_copy(
            src_ref=dst, dst_ref=dst, send_sem=ss, recv_sem=rs, device_id=at_b(b), device_id_type=MESH
        ).wait_recv()

    def sent(src, ss, rs):
        pltpu.make_async_remote_copy(
            src_ref=src, dst_ref=src, send_sem=ss, recv_sem=rs, device_id=at_b(b), device_id_type=MESH
        ).wait_send()

    def slab(p):
        return x.at[p // 2, pl.ds(pl.multiple_of(half * (p % 2), half), half)]

    barrier = pltpu.get_barrier_semaphore()
    for i in range(1, N):
        pl.semaphore_signal(barrier, inc=1, device_id=at_b((b + i) % N), device_id_type=MESH)
        pl.semaphore_signal(barrier, inc=1, device_id=at_z((z + i) % N), device_id_type=MESH)
    for i in range(1, Q):
        pl.semaphore_signal(barrier, inc=1, device_id=at_q((q + i) % Q), device_id_type=MESH)
    pl.semaphore_wait(barrier, 2 * (N - 1) + Q - 1)

    for i in range(1, N):
        p = (b + i) % N
        push(slab(p), t1.at[b], s_t1.at[i], r_t1.at[i], at_b(p))
    sib = (q // 2) * 2 + (1 - q % 2)
    par = (q + 2) % Q
    push(x, xq.at[:, q], s_q.at[0], r_q.at[0], at_q(sib))
    push(x, xq.at[:, q], s_q.at[1], r_q.at[1], at_q(par))
    t1[b] = slab(b)[...]
    xq[:, q] = x[...]
    hb[z] = x[...]

    for i in range(N):
        bb = (b + N - i) % N
        if i > 0:
            arrive(t1.at[bb], s_t1.at[i], r_t1.at[i])
        j = (bb + N - z) % N

        @pl.when(j != 0)
        def _():
            send(t1.at[bb], t2.at[z], s_t2.at[j], r_t2.at[j], at_z(bb))

        @pl.when(j == 0)
        def _():
            t2[z] = t1[bb]

    up, down = at_z((z + 1) % N), at_z((z + N - 1) % N)
    push(x, hb.at[z], s_h.at[0], r_h.at[0], up)
    push(x, hb.at[z], s_h.at[1], r_h.at[1], down)

    def pass_history(step):
        lo = hb.at[(z + N - step) % N]
        hi = hb.at[(z + step) % N]
        if step < 4:
            arrive(lo, s_h.at[2 * step - 2], r_h.at[2 * step - 2])
            arrive(hi, s_h.at[2 * step - 1], r_h.at[2 * step - 1])
        else:
            first, second = lo.at[pl.ds(0, 2)], hi.at[pl.ds(2, 2)]
            arrive(first, s_h.at[2 * step - 2], r_h.at[2 * step - 2])
            arrive(second, s_h.at[2 * step - 1], r_h.at[2 * step - 1])
            return
        if step < 3:
            push(lo, lo, s_h.at[2 * step], r_h.at[2 * step], up)
            push(hi, hi, s_h.at[2 * step + 1], r_h.at[2 * step + 1], down)
        else:
            push(lo.at[pl.ds(0, 2)], lo.at[pl.ds(0, 2)], s_h.at[6], r_h.at[6], up)
            push(hi.at[pl.ds(2, 2)], hi.at[pl.ds(2, 2)], s_h.at[7], r_h.at[7], down)

    for i in range(N):
        zz = (z + N - i) % N
        if i > 0:
            arrive(t2.at[zz], s_t2.at[i], r_t2.at[i])
        j = (zz + N - b) % N

        @pl.when(j != 0)
        def _():
            send(t2.at[zz], f.at[b], s_t3.at[j], r_t3.at[j], at_b(zz))

        @pl.when(j == 0)
        def _():
            f[b] = t2[zz]

    arrive(xq.at[:, par], s_q.at[1], r_q.at[1])
    push(xq.at[:, par], xq.at[:, par], s_q.at[2], r_q.at[2], at_q(sib))
    arrive(xq.at[:, sib], s_q.at[0], r_q.at[0])
    arrive(xq.at[:, (sib + 2) % Q], s_q.at[2], r_q.at[2])

    one_hot = (
        lax.broadcasted_iota(jnp.int32, (rows, cols), 1)
        == lax.broadcasted_iota(jnp.int32, (rows, cols), 0) + rows * q
    ).astype(F32).astype(BF16)
    base = [dot(one_hot, xq[c].reshape(cols, cols), NT) for c in range(4)]
    for i in range(1, N):
        p = (b + N - i) % N
        arrive(f.at[p], s_t3.at[i], r_t3.at[i])
    mirror = f[...].reshape(4, rows, cols).astype(F32)
    weight = w[...]

    def energy(br, bi, mr, mi):
        sr = br * br - bi * bi
        si = 2.0 * br * bi
        return [((sr * mr - si * mi) * weight).astype(BF16), ((sr * mi + si * mr) * weight).astype(BF16)]

    parts = energy(base[2], base[3], mirror[0], mirror[1]) + energy(base[0], base[1], mirror[2], mirror[3])
    sigma = jnp.concatenate(parts, axis=0)
    eye = (
        lax.broadcasted_iota(jnp.int32, (cols, cols), 1) == lax.broadcasted_iota(jnp.int32, (cols, cols), 0)
    ).astype(F32).astype(BF16)
    sg[b] = dot(eye, sigma, NT).astype(BF16)

    def place(dx, dy):
        return ((xh + dx) % 2) * Y + (y + dy) % Y

    nxt, prv, opp = place(0, 1), place(0, 3), place(1, 0)

    def share(src_place, k):
        push(sg.at[src_place], sg.at[src_place], s_s.at[k], r_s.at[k], at_b(nxt))
        push(sg.at[src_place], sg.at[src_place], s_s.at[k + 1], r_s.at[k + 1], at_b(prv))

    def share_far(dx, k):
        before, after = place(dx, 3), place(dx, 1)
        arrive(sg.at[before], s_s.at[k], r_s.at[k])
        one = sg.at[before, pl.ds(0, cols // 2)]
        push(one, one, s_s.at[k + 2], r_s.at[k + 2], at_b(nxt))
        arrive(sg.at[after], s_s.at[k + 1], r_s.at[k + 1])
        two = sg.at[after, pl.ds(cols // 2, cols // 2)]
        push(two, two, s_s.at[k + 3], r_s.at[k + 3], at_b(prv))

    def arrive_far(dx, k):
        far = place(dx, 2)
        arrive(sg.at[far, pl.ds(0, cols // 2)], s_s.at[k + 2], r_s.at[k + 2])
        arrive(sg.at[far, pl.ds(cols // 2, cols // 2)], s_s.at[k + 3], r_s.at[k + 3])

    push(sg.at[b], sg.at[b], s_s.at[0], r_s.at[0], at_b(opp))
    share(b, 1)
    pass_history(1)
    arrive(sg.at[opp], s_s.at[0], r_s.at[0])
    share(opp, 5)
    pass_history(2)
    share_far(0, 1)
    pass_history(3)
    share_far(1, 5)
    pass_history(4)

    before = jnp.zeros((4, ORB, cols), F32)
    for zz in range(N - 1):
        tile = hb[zz].astype(F32)
        total = tile[:, 0:ORB]
        for k in range(1, times):
            total = total + tile[:, k * ORB:(k + 1) * ORB]
        before = before + jnp.where(zz < z, total, 0.0)
    ax_s[...] = before.astype(BF16)
    for i in range(1, Q):
        push(ax_s, ax_r.at[q], s_ax.at[i], r_ax.at[i], at_q((q + i) % Q))

    @pl.when(q == 0)
    def _():
        edge = hb[0, :, 0:ORB]
        ed_r[...] = edge
        for i in range(1, Q):
            send(hb.at[0, :, pl.ds(0, ORB)], ed_r, s_ed.at[i], r_ed.at[0], at_q(i))

    def multiply(bb, first):
        tile = hb[bb]
        lr, li, gr, gi = tile[0], tile[1], tile[2], tile[3]
        bm[:, 0:cols] = jnp.concatenate([lr, -li, -gr, gi], axis=0)
        bm[:, cols:2 * cols] = jnp.concatenate([li, lr, -gi, -gr], axis=0)
        prod = dot(sg[bb], bm[...])
        if first:
            acc[...] = prod
        else:
            acc[...] += prod

    multiply(b, True)
    multiply(opp, False)
    multiply(prv, False)
    multiply(nxt, False)
    multiply(place(1, 3), False)
    multiply(place(1, 1), False)
    arrive_far(0, 1)
    multiply(place(0, 2), False)
    arrive_far(1, 5)
    multiply(place(1, 2), False)

    run = jnp.zeros((ORB, 2 * cols), F32)
    for k in range(Q):
        for m in range(times):
            at = (k * times + m) * ORB
            term = acc[pl.ds(at, ORB), :]
            acc[pl.ds(at, ORB), :] = run
            rs_s[k, pl.ds(m * ORB, ORB), :] = run.astype(BF16)
            run = run + term
    zt_s[...] = run.astype(BF16)
    for i in range(1, N):
        @pl.when(z + i < N)
        def _():
            send(zt_s, zt_r.at[z], s_zt.at[i], r_zt.at[i], at_z(z + i))
    for i in range(1, Q):
        to = (q + i) % Q
        push(rs_s.at[to], rs_r.at[q], s_rs.at[i], r_rs.at[i], at_q(to))

    carry = jnp.zeros((ORB, 2 * cols), F32)
    for i in range(1, N):
        @pl.when(z - i >= 0)
        def _():
            arrive(zt_r.at[z - i], s_zt.at[i], r_zt.at[i])
    for zz in range(N - 1):
        carry = carry + jnp.where(zz < z, zt_r[zz].astype(F32), 0.0)
    a_s[...] = carry.astype(BF16)
    for i in range(1, Q):
        push(a_s, a_r.at[q], s_a.at[i], r_a.at[i], at_q((q + i) % Q))

    for i in range(1, Q):
        arrive(ax_r.at[(q + Q - i) % Q], s_ax.at[i], r_ax.at[i])
        before = before + ax_r[(q + Q - i) % Q].astype(F32)

    @pl.when(q != 0)
    def _():
        arrive(ed_r, s_ed.at[0], r_ed.at[0])

    for qq in range(Q - 1):
        tile = xq[:, qq].astype(F32)
        total = tile[:, 0:ORB]
        for k in range(1, times):
            total = total + tile[:, k * ORB:(k + 1) * ORB]
        before = before + jnp.where(qq < q, total, 0.0)
    own = x[...].astype(F32)
    hopped = []
    hop = h3[...]
    for c in range(4):
        level = before[c]
        levels = [level]
        for k in range(times - 1):
            level = level + own[c, k * ORB:(k + 1) * ORB]
            levels.append(level)
        level = jnp.concatenate(levels, axis=0)
        high = level.astype(BF16)
        low = (level - high.astype(F32)).astype(BF16)
        hopped.append(dot(hop, high) + dot(hop, low))

    coll = acc[pl.ds(pl.multiple_of(q * rows, rows), rows), :]
    for i in range(1, Q):
        arrive(rs_r.at[(q + Q - i) % Q], s_rs.at[i], r_rs.at[i])
        coll = coll + rs_r[(q + Q - i) % Q].astype(F32)
    for i in range(1, Q):
        arrive(a_r.at[(q + Q - i) % Q], s_a.at[i], r_a.at[i])
        carry = carry + a_r[(q + Q - i) % Q].astype(F32)
    coll = dt * (coll + jnp.concatenate([carry] * times, axis=0))
    for c in range(4):
        edge = jnp.concatenate([ed_r[c].astype(F32)] * times, axis=0)
        if c % 2 == 0:
            new = edge + dt * (hopped[c + 1] + coll[:, cols:])
        else:
            new = edge - dt * (hopped[c - 1] + coll[:, :cols])
        out[c] = new.astype(BF16)

    for copy in started:
        copy.wait_send()
    for i in range(N):
        bb = (b + N - i) % N
        j = (bb + N - z) % N

        @pl.when(j != 0)
        def _():
            sent(t1.at[bb], s_t2.at[j], r_t2.at[j])

        zz = (z + N - i) % N
        k = (zz + N - b) % N

        @pl.when(k != 0)
        def _():
            sent(t2.at[zz], s_t3.at[k], r_t3.at[k])
    for i in range(1, N):
        @pl.when(z + i < N)
        def _():
            sent(zt_s, s_zt.at[i], r_zt.at[i])

    @pl.when(q == 0)
    def _():
        for i in range(1, Q):
            sent(hb.at[0, :, pl.ds(0, ORB)], s_ed.at[i], r_ed.at[0])


def one_step(x, w, h3, dt):
    rows, cols = x.shape[1:]
    dma = pltpu.SemaphoreType.DMA
    sems = [8, 8, 8, 8, 8, 8, 3, 3, 8, 8, 9, 9, 4, 4, 8, 8, 4, 4, 4, 1, 4, 4]
    return pl.pallas_call(
        functools.partial(kernel, dt),
        out_shape=jax.ShapeDtypeStruct(x.shape, BF16),
        in_specs=[pl.BlockSpec(memory_space=pltpu.VMEM)] * 3,
        out_specs=pl.BlockSpec(memory_space=pltpu.VMEM),
        scratch_shapes=[
            pltpu.VMEM((4, Q, rows, cols), BF16),
            pltpu.VMEM((N, rows // 2, cols), BF16),
            pltpu.VMEM((N, rows // 2, cols), BF16),
            pltpu.VMEM((N, rows // 2, cols), BF16),
            pltpu.VMEM((N, cols, cols), BF16),
            pltpu.VMEM((N, 4, rows, cols), BF16),
            pltpu.VMEM((cols, 2 * cols), F32),
            pltpu.VMEM((cols, 2 * cols), BF16),
            pltpu.VMEM((Q, rows, 2 * cols), BF16),
            pltpu.VMEM((Q, rows, 2 * cols), BF16),
            pltpu.VMEM((ORB, 2 * cols), BF16),
            pltpu.VMEM((N, ORB, 2 * cols), BF16),
            pltpu.VMEM((4, ORB, cols), BF16),
            pltpu.VMEM((Q, 4, ORB, cols), BF16),
            pltpu.VMEM((4, ORB, cols), BF16),
            pltpu.VMEM((ORB, 2 * cols), BF16),
            pltpu.VMEM((Q, ORB, 2 * cols), BF16),
        ] + [dma((n,)) for n in sems],
        compiler_params=pltpu.CompilerParams(
            collective_id=0, has_side_effects=True, vmem_limit_bytes=48 * 1024 * 1024
        ),
        cost_estimate=pl.CostEstimate(flops=2 * 4 * 768 * 768 * 768, bytes_accessed=10**6, transcendentals=0),
    )(x, w, h3)


def per_device(lesser, greater, hopping, coupling):
    rows, cols = lesser.shape[1:]
    dt = 3.0 / (rows * N * Q // ORB)
    w = jnp.tile(coupling, rows // ORB)[:, None] * jnp.tile(coupling, cols // ORB)[None, :]
    h3 = jnp.kron(jnp.eye(rows // ORB, dtype=hopping.dtype), hopping)
    x = jnp.concatenate([lesser, greater], axis=0)
    for _ in range(STEPS):
        x = one_step(x, w, h3, dt)
    return x[:2], x[2:]


def solution(mesh):
    in_specs = (P(None, "trow", "tcol"), P(None, "trow", "tcol"), P(), P())
    out_specs = (P(None, "trow", "tcol"), P(None, "trow", "tcol"))
    return jax.shard_map(per_device, mesh=mesh, in_specs=in_specs, out_specs=out_specs, check_vma=False)
```

time: 1090 us -> 132 us (0.12)
  the two profiles are of different devices: /device:TPU:231 before, /device:TPU:1 now
where the time goes in v1:
time: 132 us; the launch traced here: 131 us
  Pallas kernels  127 us (96%)
  local copies, waits for them, and re-layouts  2.99 us (2%)
    pallas_call x2, Pallas kernels, one_step(): pl.pallas_call(functools.partial(kernel, dt), out_shape=jax.ShapeDtypeStr...  127 us

profile of v1, /device:TPU:1, one launch (start us, length us, event | category | flops | bytes accessed | tf_op | source)
XLA Modules:
  0.0 130.5 jit_solution(4931329575677562689)
XLA Ops:
  0.6 0.0 copy-start.3
  0.7 0.6 copy-done.3
  1.3 0.1 mul.41
  1.4 0.0 copy-start.2
  1.4 0.1 mul.43
  1.5 0.6 copy-done.2
  2.1 0.0 copy-start.1
  2.1 0.1 broadcast_multiply_fusion.1
  2.2 0.0 copy-start
  2.2 0.1 mul.49.h3
  2.3 0.1 broadcast_multiply_fusion.w
  2.4 0.6 copy-done.1
  3.0 0.1 copy-done
  3.2 64.9 %shard_map.59.x = bf16[4,96,384]{2,1,0:T(8,128)(2,1)S(1)} custom-call(bf16[4,96,384]{2,1,0:T(8,128)(2,1)S(1)} %pad_maximum_fusion.x, f32[96,384]{1,0:T(8,128)S(1)} %broadcast_multiply_fusion.w, bf16[96,96]{1,0:T(8,128)(2,1)S(1)} %mul.49.h3), custom_call_target="tpu_custom_call" | custom-call | flops 3623878656 | bytes 1000000 | tf_op jit(solution)/shard_map/pallas_call | solution.py:349
  68.0 61.7 %shard_map.60 = bf16[4,96,384]{2,1,0:T(8,128)(2,1)S(1)} custom-call(bf16[4,96,384]{2,1,0:T(8,128)(2,1)S(1)} %shard_map.59.x, f32[96,384]{1,0:T(8,128)S(1)} %broadcast_multiply_fusion.w, bf16[96,96]{1,0:T(8,128)(2,1)S(1)} %mul.49.h3), custom_call_target="tpu_custom_call" | custom-call | flops 3623878656 | bytes 1000000 | tf_op jit(solution)/shard_map/pallas_call | solution.py:349
  129.8 0.7 fusion.1
  (4 shorter events, 0.0 us)
Async XLA Ops:
  0.6 0.7 copy-start.3
  1.4 0.7 copy-start.2
  2.1 0.9 copy-start.1
  2.2 0.9 copy-start

commit v2 on v0

v2 whole, which is shorter than its diff:
```python
import functools

import jax
import jax.numpy as jnp
from jax import lax
from jax.experimental import pallas as pl
from jax.experimental.pallas import tpu as pltpu
from jax.sharding import PartitionSpec as P

MESH = pl.DeviceIdType.MESH
ORB = 32
STEPS = 2
N = 8
Q = 4
Y = 4
J = 3
HALF = ORB // 2
F32 = jnp.float32
BF16 = jnp.bfloat16
NT = (((1,), (1,)), ((), ()))
NN = (((1,), (0,)), ((), ()))
PIECES = ((0, 0, Q * J), (1, 0, Q * J), (2, 0, Q), (2, Q, Q), (2, 2 * Q, Q))


def dot(a, b, dims=NN):
    return lax.dot_general(a, b, dims, preferred_element_type=F32)


def kernel(
    dt, lesser, greater, w, h3, out_l, out_g,
    x, xq, t1, f, sg, hb, bm, acc, pre, hop, zs_s, zs_r, cs, rs_s, rs_r, ax_s, ax_r, ed,
    s_in, s_t1, r_t1, s_t2, r_t2, s_q, r_q, s_h, r_h, s_g, r_g,
    s_zs, r_zs, s_cs, r_cs, s_rs, r_rs, s_ax, r_ax, s_ed, r_ed,
):
    cols = x.shape[-1]
    wide = 4 * ORB
    r = lax.axis_index("trow")
    b = lax.axis_index("tcol")
    z, q = r // Q, r % Q
    xh, y = b // Y, b % Y

    def at(zz, qq, bb):
        return {"trow": zz * Q + qq, "tcol": bb}

    drains = []

    def copy_of(src, dst, ss, rs, where):
        return pltpu.make_async_remote_copy(
            src_ref=src, dst_ref=dst, send_sem=ss, recv_sem=rs, device_id=where, device_id_type=MESH
        )

    def push(src, dst, ss, rs, where):
        copy = copy_of(src, dst, ss, rs, where)
        copy.start()
        drains.append(copy.wait_send)

    def push_if(cond, src, dst, ss, rs, where):
        @pl.when(cond)
        def _():
            copy_of(src, dst, ss, rs, where).start()

        def drain():
            @pl.when(cond)
            def _():
                copy_of(src, dst, ss, rs, where).wait_send()

        drains.append(drain)

    def arrive(dst, rs):
        copy_of(dst, dst, s_in.at[0], rs, at(z, q, b)).wait_recv()

    def place(dx, dy):
        return ((xh + dx) % 2) * Y + (y + dy) % Y

    sib = (q // 2) * 2 + (1 - q % 2)
    par = (q + 2) % Q
    dia = (sib + 2) % Q
    up, down = at((z + 1) % N, q, b), at((z + N - 1) % N, q, b)


    def mirror_out(st, j):
        for i in range(1, N):
            p = (b + i) % N
            k = (st * J + j) * N + i
            src = x.at[st, p // 2, j, pl.ds(pl.multiple_of(HALF * (p % 2), HALF), HALF)]
            push(src, t1.at[st, j, b], s_t1.at[k], r_t1.at[k], at(z, q, p))
        t1[st, j, b] = x[st, b // 2, j, pl.ds(pl.multiple_of(HALF * (b % 2), HALF), HALF)]

    def mirror_on(st, j):
        base = (st * J + j) * N
        for i in range(N):
            bb = (b + N - i) % N
            if i > 0:
                arrive(t1.at[st, j, bb], r_t1.at[base + i])
            here = jnp.logical_and(bb == z, b == z)
            push_if(
                jnp.logical_not(here), t1.at[st, j, bb], f.at[st, j, b], s_t2.at[base + i], r_t2.at[base + b], at(bb, q, z)
            )

            @pl.when(here)
            def _():
                f[st, j, b] = t1[st, j, bb]

    def mirror_in(st, j):
        base = (st * J + j) * N
        for i in range(N):
            p = (b + i) % N
            if i > 0:
                arrive(f.at[st, j, p], r_t2.at[base + p])
            else:
                @pl.when(b != z)
                def _():
                    arrive(f.at[st, j, p], r_t2.at[base + p])

    def quad_out(st, j):
        k = (st * J + j) * 3
        push(x.at[st, :, j], xq.at[st, :, q, j], s_q.at[k + 1], r_q.at[k + 1], at(z, par, b))
        push(x.at[st, :, j], xq.at[st, :, q, j], s_q.at[k], r_q.at[k], at(z, sib, b))
        xq[st, :, q, j] = x[st, :, j]

    def quad_on(st, j):
        k = (st * J + j) * 3
        arrive(xq.at[st, :, par, j], r_q.at[k + 1])
        push(xq.at[st, :, par, j], xq.at[st, :, par, j], s_q.at[k + 2], r_q.at[k + 2], at(z, sib, b))

    def quad_in(st, j):
        k = (st * J + j) * 3
        arrive(xq.at[st, :, sib, j], r_q.at[k])
        arrive(xq.at[st, :, dia, j], r_q.at[k + 2])

    def history(st, s, j):
        base = (st * J + j) * 8
        lo, hi = (z + N - s) % N, (z + s) % N
        first, second = (pl.ds(0, 2), pl.ds(2, 2)) if s >= 3 else (pl.ds(0, 4), pl.ds(0, 4))
        if s > 0:
            got = (pl.ds(0, 2), pl.ds(2, 2)) if s == 4 else (pl.ds(0, 4), pl.ds(0, 4))
            arrive(hb.at[st, lo, got[0], j], r_h.at[base + 2 * s - 2])
            arrive(hb.at[st, hi, got[1], j], r_h.at[base + 2 * s - 1])
        if s < 4:
            one, two = hb.at[st, lo, first, j], hb.at[st, hi, second, j]
            from_one, from_two = (x.at[st, :, j], x.at[st, :, j]) if s == 0 else (one, two)
            push(from_one, one, s_h.at[base + 2 * s], r_h.at[base + 2 * s], up)
            push(from_two, two, s_h.at[base + 2 * s + 1], r_h.at[base + 2 * s + 1], down)

    def tile(st, piece, bb):
        k, m, n = PIECES[piece]
        return sg.at[st, k, pl.ds(ORB * (1 + m), ORB * n), pl.ds(pl.multiple_of(wide * bb, wide), wide)]

    def give(st, piece, way, bb, to):
        k = (st * len(PIECES) + piece) * 7 + way
        push(tile(st, piece, bb), tile(st, piece, bb), s_g.at[k], r_g.at[k], at(z, q, to))

    def take(st, piece, way, bb):
        arrive(tile(st, piece, bb), r_g.at[(st * len(PIECES) + piece) * 7 + way])

    def give_own(st, piece):
        give(st, piece, 0, b, place(1, 0))
        give(st, piece, 1, b, place(0, 1))
        give(st, piece, 2, b, place(0, 3))

    def give_partner(st, piece):
        take(st, piece, 0, place(1, 0))
        give(st, piece, 3, place(1, 0), place(0, 1))
        give(st, piece, 4, place(1, 0), place(0, 3))

    def give_far(st, piece):
        take(st, piece, 1, place(0, 3))
        give(st, piece, 5, place(0, 3), place(0, 1))

    def give_far_partner(st, piece):
        take(st, piece, 4, place(1, 1))
        give(st, piece, 6, place(1, 1), place(0, 3))

    def take_rest(st, piece):
        take(st, piece, 2, place(0, 1))
        take(st, piece, 3, place(1, 3))
        take(st, piece, 5, place(0, 2))
        take(st, piece, 6, place(1, 2))


    into = [
        pltpu.make_async_copy(lesser, x.at[0, pl.ds(0, 2)], s_in.at[1]),
        pltpu.make_async_copy(greater, x.at[0, pl.ds(2, 2)], s_in.at[2]),
    ]
    for copy in into:
        copy.start()
    barrier = pltpu.get_barrier_semaphore()
    for i in range(1, N):
        pl.semaphore_signal(barrier, inc=1, device_id=at((z + i) % N, q, b), device_id_type=MESH)
        pl.semaphore_signal(barrier, inc=1, device_id=at(z, q, (b + i) % N), device_id_type=MESH)
    for i in range(1, Q):
        pl.semaphore_signal(barrier, inc=1, device_id=at(z, (q + i) % Q, b), device_id_type=MESH)
    for i in range(N):
        bb = (b + i) % N

        @pl.when(jnp.logical_and(bb != z, b != z))
        def _():
            pl.semaphore_signal(barrier, inc=1, device_id=at(bb, q, z), device_id_type=MESH)
            if i > 0:
                pl.semaphore_signal(barrier, inc=1, device_id=at(b, q, bb), device_id_type=MESH)

    row = lax.broadcasted_iota(jnp.int32, (ORB + cols, cols), 0) - ORB
    col = lax.broadcasted_iota(jnp.int32, (ORB + cols, cols), 1)
    when = jnp.where(row < 0, Q * J, ((row >> 5) & 3) * J + (row >> 7))
    pre[...] = jnp.where(jnp.logical_and((row & 31) == (col & 31), (col >> 5) < when), 1.0, 0.0).astype(BF16)
    one_hot = (
        lax.broadcasted_iota(jnp.int32, (J * ORB, cols), 1)
        == lax.broadcasted_iota(jnp.int32, (J * ORB, cols), 0) + J * ORB * q
    ).astype(F32).astype(BF16)
    for copy in into:
        copy.wait()
    hb[0, z] = x[0]

    greeted = 2 * (N - 1) + Q - 1

    @pl.when(b == z)
    def _():
        pl.semaphore_wait(barrier, greeted)

    @pl.when(b != z)
    def _():
        pl.semaphore_wait(barrier, greeted + 2 * N - 3)

    for j in range(J):
        mirror_out(0, j)
    history(0, 0, 0)
    history(0, 0, 1)
    for j in range(J):
        quad_out(0, j)

    for st in range(STEPS):
        mirror_on(st, 0)
        if st == 0:
            history(st, 0, 2)
        mirror_on(st, 1)
        mirror_on(st, 2)
        history(st, 1, 0)
        for j in range(J):
            quad_on(st, j)
        history(st, 1, 1)
        for j in range(J):
            quad_in(st, j)
        base = [dot(one_hot, xq[st, c].reshape(cols, cols), NT) for c in range(4)]

        for j in range(J):
            mirror_in(st, j)
            part = slice(j * ORB, (j + 1) * ORB)
            mir = f[st, j].reshape(4, ORB, cols).astype(F32)
            weight = w[part, :]

            def energy(br, bi, mr, mi):
                sr = br * br - bi * bi
                si = 2.0 * br * bi
                return [((sr * mr - si * mi) * weight).astype(BF16), ((sr * mi + si * mr) * weight).astype(BF16)]

            sigma = jnp.concatenate(
                energy(base[2][part], base[3][part], mir[0], mir[1])
                + energy(base[0][part], base[1][part], mir[2], mir[3]),
                axis=0,
            )
            summed = dot(pre[...], sigma, NT).astype(BF16)
            sg[st, j, pl.ds(ORB, cols), pl.ds(pl.multiple_of(wide * b, wide), wide)] = summed[ORB:]
            zs_s[st, :, j * wide:(j + 1) * wide] = summed[:ORB]
            for piece, (k, _, _) in enumerate(PIECES):
                if k == j:
                    give_own(st, piece)

        for i in range(1, N):
            push_if(
                z + i < N, zs_s.at[st], zs_r.at[st, z], s_zs.at[st * N + i], r_zs.at[st * N + i], at((z + i) % N, q, b)
            )

        history(st, 1, 2)
        give_partner(st, 0)
        give_far(st, 0)
        history(st, 2, 0)
        give_partner(st, 1)
        give_far(st, 1)
        history(st, 2, 1)

        carry = jnp.zeros((ORB, cols), F32)
        for i in range(1, N):
            @pl.when(z - i >= 0)
            def _():
                arrive(zs_r.at[st, (z + N - i) % N], r_zs.at[st * N + i])
        for zz in range(N - 1):
            carry = carry + jnp.where(zz < z, zs_r[st, zz].astype(F32), 0.0)
        cs[st, b] = carry.astype(BF16)
        for i in range(1, N):
            k = st * N + i
            push(cs.at[st, b], cs.at[st, b], s_cs.at[k], r_cs.at[k], at(z, q, (b + i) % N))

        give_far_partner(st, 0)
        history(st, 2, 2)
        for piece in (2, 3, 4):
            give_partner(st, piece)
            give_far(st, piece)
        history(st, 3, 0)
        give_far_partner(st, 1)
        history(st, 3, 1)
        history(st, 3, 2)
        for piece in (2, 3, 4):
            give_far_partner(st, piece)
        for j in range(J):
            history(st, 4, j)

        def build(zz, before):
            got = hb[st, zz]
            for j in range(J):
                lr, li, gr, gi = got[0, j], got[1, j], got[2, j], got[3, j]
                rows = pl.ds(pl.multiple_of(wide * zz, wide), wide)
                bm[j, rows, 0:cols] = jnp.concatenate([lr, -li, -gr, gi], axis=0)
                bm[j, rows, cols:2 * cols] = jnp.concatenate([li, lr, -gi, -gr], axis=0)
            total = jnp.sum(got.astype(F32), axis=1)
            return before + jnp.where(zz < z, total, 0.0)

        before = lax.fori_loop(0, N, build, jnp.zeros((4, ORB, cols), F32))
        ax_s[st] = before.astype(BF16)
        for i in range(1, Q):
            k = st * Q + i
            push(ax_s.at[st], ax_r.at[st, q], s_ax.at[k], r_ax.at[k], at(z, (q + i) % Q, b))
        if st == 0:
            @pl.when(q == 0)
            def _():
                ed[...] = hb[0, 0, :, 0]

            for i in range(1, Q):
                push_if(q == 0, hb.at[0, 0, :, 0], ed, s_ed.at[i], r_ed.at[0], at(z, i, b))

        for qq in range(Q - 1):
            total = jnp.sum(xq[st, :, qq].astype(F32), axis=1)
            before = before + jnp.where(qq < q, total, 0.0)
        for i in range(1, Q):
            arrive(ax_r.at[st, (q + Q - i) % Q], r_ax.at[st * Q + i])
            before = before + ax_r[st, (q + Q - i) % Q].astype(F32)
        for c in range(4):
            level = before[c]
            levels = [level]
            for j in range(J - 1):
                level = level + x[st, c, j].astype(F32)
                levels.append(level)
            level = jnp.concatenate(levels, axis=0)
            high = level.astype(BF16)
            low = (level - high.astype(F32)).astype(BF16)
            hop[c] = dot(h3[...], high) + dot(h3[...], low)

        for i in range(1, N):
            arrive(cs.at[st, (b + N - i) % N], r_cs.at[st * N + i])
        for bb in range(N):
            for j in range(J):
                sg[st, j, 0:ORB, bb * wide:(bb + 1) * wide] = cs[st, bb, :, j * wide:(j + 1) * wide]
        take_rest(st, 0)
        acc[...] = dot(sg[st, 0], bm[0])
        take_rest(st, 1)
        acc[...] += dot(sg[st, 1], bm[1])
        lead = None
        for m in range(J):
            take_rest(st, 2 + m)
            lo, hi = (0 if m == 0 else ORB + m * wide), ORB + (m + 1) * wide
            part = acc[lo:hi, :] + dot(sg[st, 2, lo:hi, :], bm[2])
            if m == 0:
                lead = jnp.concatenate([part[:ORB]] * Q, axis=0)
                part = part[ORB:]
            part = part + lead
            acc[ORB + m * wide:hi, :] = part
            rs_s[st, m] = part.reshape(Q, ORB, 2 * cols).astype(BF16)
            for i in range(1, Q):
                to = (q + i) % Q
                k = (st * J + m) * Q + i
                push(rs_s.at[st, m, to], rs_r.at[st, m, q], s_rs.at[k], r_rs.at[k], at(z, to, b))

        if st == 0:
            @pl.when(q != 0)
            def _():
                arrive(ed, r_ed.at[0])

        for m in range(J):
            coll = acc[pl.ds(pl.multiple_of(ORB + m * wide + ORB * q, ORB), ORB), :]
            for i in range(1, Q):
                arrive(rs_r.at[st, m, (q + Q - i) % Q], r_rs.at[(st * J + m) * Q + i])
                coll = coll + rs_r[st, m, (q + Q - i) % Q].astype(F32)
            coll = dt * coll
            for c in range(4):
                edge = ed[c].astype(F32)
                if c % 2 == 0:
                    new = edge + dt * (hop[c + 1, m * ORB:(m + 1) * ORB] + coll[:, cols:])
                else:
                    new = edge - dt * (hop[c - 1, m * ORB:(m + 1) * ORB] + coll[:, :cols])
                new = new.astype(BF16)
                if st + 1 < STEPS:
                    x[st + 1, c, m] = new
                elif c < 2:
                    out_l[c, m] = new
                else:
                    out_g[c - 2, m] = new
            if st + 1 < STEPS:
                hb[st + 1, z, :, m] = x[st + 1, :, m]
                mirror_out(st + 1, m)
                quad_out(st + 1, m)
                history(st + 1, 0, m)

    for drain in drains:
        drain()


def per_device(lesser, greater, hopping, coupling):
    rows, cols = lesser.shape[1:]
    dt = 3.0 / (rows * N * Q // ORB)
    w = jnp.tile(coupling, rows // ORB)[:, None] * jnp.tile(coupling, cols // ORB)[None, :]
    h3 = jnp.kron(jnp.eye(rows // ORB, dtype=hopping.dtype), hopping)
    part = (2, J, ORB, cols)
    wide = 4 * ORB

    def dma(n):
        return pltpu.SemaphoreType.DMA((n,))

    one = [dma(3)]
    pairs = [STEPS * J * N, STEPS * J * N, STEPS * J * 3, STEPS * J * 8, STEPS * len(PIECES) * 7]
    pairs += [STEPS * N, STEPS * N, STEPS * J * Q, STEPS * Q, Q]
    for n in pairs:
        one += [dma(n), dma(n)]
    outs = pl.pallas_call(
        functools.partial(kernel, dt),
        out_shape=[jax.ShapeDtypeStruct(part, BF16)] * 2,
        in_specs=[pl.BlockSpec(memory_space=pl.ANY)] * 2 + [pl.BlockSpec(memory_space=pltpu.VMEM)] * 2,
        out_specs=[pl.BlockSpec(memory_space=pltpu.VMEM)] * 2,
        scratch_shapes=[
            pltpu.VMEM((STEPS, 4, J, ORB, cols), BF16),
            pltpu.VMEM((STEPS, 4, Q, J, ORB, cols), BF16),
            pltpu.VMEM((STEPS, J, N, HALF, cols), BF16),
            pltpu.VMEM((STEPS, J, N, HALF, cols), BF16),
            pltpu.VMEM((STEPS, J, ORB + cols, N * wide), BF16),
            pltpu.VMEM((STEPS, N, 4, J, ORB, cols), BF16),
            pltpu.VMEM((J, N * wide, 2 * cols), BF16),
            pltpu.VMEM((ORB + cols, 2 * cols), F32),
            pltpu.VMEM((ORB + cols, cols), BF16),
            pltpu.VMEM((4, J * ORB, cols), F32),
            pltpu.VMEM((STEPS, ORB, cols), BF16),
            pltpu.VMEM((STEPS, N, ORB, cols), BF16),
            pltpu.VMEM((STEPS, N, ORB, cols), BF16),
            pltpu.VMEM((STEPS, J, Q, ORB, 2 * cols), BF16),
            pltpu.VMEM((STEPS, J, Q, ORB, 2 * cols), BF16),
            pltpu.VMEM((STEPS, 4, ORB, cols), BF16),
            pltpu.VMEM((STEPS, Q, 4, ORB, cols), BF16),
            pltpu.VMEM((4, ORB, cols), BF16),
        ] + one,
        compiler_params=pltpu.CompilerParams(
            collective_id=0, has_side_effects=True, vmem_limit_bytes=56 * 1024 * 1024
        ),
        cost_estimate=pl.CostEstimate(flops=4 * 10**9, bytes_accessed=10**6, transcendentals=0),
    )(lesser.reshape(part), greater.reshape(part), w, h3)
    return outs[0].reshape(lesser.shape), outs[1].reshape(greater.shape)


def solution(mesh):
    in_specs = (P(None, "trow", "tcol"), P(None, "trow", "tcol"), P(), P())
    out_specs = (P(None, "trow", "tcol"), P(None, "trow", "tcol"))
    return jax.shard_map(per_device, mesh=mesh, in_specs=in_specs, out_specs=out_specs, check_vma=False)
```

time: 1090 us -> 129 us (0.12)
  the two profiles are of different devices: /device:TPU:231 before, /device:TPU:1 now
where the time goes in v2:
time: 129 us
  Pallas kernels  123 us (95%)
  local copies, waits for them, and re-layouts  4.43 us (3%)
    pallas_call x1, Pallas kernels, per_device(): pl.pallas_call(functools.partial(kernel, dt), out_shape=[jax.ShapeDtypeSt...  123 us
    unnamed x8, local copies, waits for them, and re-layouts  3.54 us

profile of v2, /device:TPU:1, one launch (start us, length us, event | category | flops | bytes accessed | tf_op | source)
XLA Modules:
  0.0 129.2 jit_solution(14281915475058182543)
XLA Ops:
  0.6 0.0 copy-start.2
  0.7 0.6 copy-done.2
  1.3 0.1 mul.41
  1.4 0.0 copy-start.1
  1.4 0.1 mul.43
  1.5 0.6 copy-done.1
  2.1 0.1 broadcast_multiply_fusion.1
  2.2 0.7 mul.49.h3
  2.9 0.7 broadcast_multiply_fusion.w
  3.6 123.3 %shard_map.59 = (bf16[2,3,32,384]{3,2,1,0:T(8,128)(2,1)}, bf16[2,3,32,384]{3,2,1,0:T(8,128)(2,1)}) custom-call(bf16[2,3,32,384]{3,2,1,0:T(8,128)(2,1)} %bitcast.6, bf16[2,3,32,384]{3,2,1,0:T(8,128)(2,1)} %bitcast.7, f32[96,384]{1,0:T(8,128)} %broadcast_multiply_fusion.w, bf16[96,96]{1,0:T(8,128)(2,1)} %mul.49.h3), custom_call_target="tpu_custom_call" | custom-call | flops 4000000000 | bytes 1000000 | tf_op jit(solution)/shard_map/pallas_call | solution.py:422
  126.9 0.0 copy-start
  127.0 1.6 %copy.8 = bf16[2,96,384]{2,1,0:T(8,128)(2,1)} copy(bf16[2,96,384]{2,1,0:T(8,128)(2,1)} %bitcast.5) | data formatting | bytes 294912
  128.6 0.0 copy-done
  128.6 0.7 copy.9
  (3 shorter events, 0.0 us)
Async XLA Ops:
  0.6 0.7 copy-start.2
  1.4 0.7 copy-start.1
  126.9 1.6 %copy-start = (bf16[2,3,32,384]{3,2,1,0:T(8,128)(2,1)S(1)}, bf16[2,3,32,384]{3,2,1,0:T(8,128)(2,1)}, u32[]{:S(2)}) copy-start(bf16[2,3,32,384]{3,2,1,0:T(8,128)(2,1)} %get-tuple-element.5) | copy-start | bytes 442372

commit v3 on v2

--- a/solution.py
+++ b/solution.py
@@ -27,8 +27,8 @@
 
 
 def kernel(
-    dt, lesser, greater, w, h3, out_l, out_g,
-    x, xq, t1, f, sg, hb, bm, acc, pre, hop, zs_s, zs_r, cs, rs_s, rs_r, ax_s, ax_r, ed,
+    dt, lesser, greater, hopping, coupling, out,
+    x, xt, xq, t1, f, sg, hb, bm, acc, pre, eye, gather, w, hm, cv, before, hop, zs_s, zs_r, cs, rs_s, rs_r, ax_s, ax_r, ed,
     s_in, s_t1, r_t1, s_t2, r_t2, s_q, r_q, s_h, r_h, s_g, r_g,
     s_zs, r_zs, s_cs, r_cs, s_rs, r_rs, s_ax, r_ax, s_ed, r_ed,
 ):
@@ -44,6 +44,10 @@
 
     drains = []
 
+    def drain_now(upto):
+        for drain in upto:
+            drain()
+
     def copy_of(src, dst, ss, rs, where):
         return pltpu.make_async_remote_copy(
             src_ref=src, dst_ref=dst, send_sem=ss, recv_sem=rs, device_id=where, device_id_type=MESH
@@ -72,9 +76,6 @@
     def place(dx, dy):
         return ((xh + dx) % 2) * Y + (y + dy) % Y
 
-    sib = (q // 2) * 2 + (1 - q % 2)
-    par = (q + 2) % Q
-    dia = (sib + 2) % Q
     up, down = at((z + 1) % N, q, b), at((z + N - 1) % N, q, b)
 
 
@@ -112,21 +113,20 @@
                 def _():
                     arrive(f.at[st, j, p], r_t2.at[base + p])
 
-    def quad_out(st, j):
-        k = (st * J + j) * 3
-        push(x.at[st, :, j], xq.at[st, :, q, j], s_q.at[k + 1], r_q.at[k + 1], at(z, par, b))
-        push(x.at[st, :, j], xq.at[st, :, q, j], s_q.at[k], r_q.at[k], at(z, sib, b))
-        xq[st, :, q, j] = x[st, :, j]
-
-    def quad_on(st, j):
-        k = (st * J + j) * 3
-        arrive(xq.at[st, :, par, j], r_q.at[k + 1])
-        push(xq.at[st, :, par, j], xq.at[st, :, par, j], s_q.at[k + 2], r_q.at[k + 2], at(z, sib, b))
-
-    def quad_in(st, j):
-        k = (st * J + j) * 3
-        arrive(xq.at[st, :, sib, j], r_q.at[k])
-        arrive(xq.at[st, :, dia, j], r_q.at[k + 2])
+    def quad_out(st):
+        for c in range(4):
+            xt[st, :, c, :, 0:J * ORB] = dot(eye[...], x[st, c].reshape(J * ORB, cols), NT).astype(BF16).reshape(Q, J * ORB, J * ORB)
+        lanes = pl.ds(pl.multiple_of(wide * q, wide), wide)
+        for i in range(1, Q):
+            k = st * Q + i
+            to = (q + i) % Q
+            push(xt.at[st, to], xq.at[st, :, :, lanes], s_q.at[k], r_q.at[k], at(z, to, b))
+        xq[st, :, :, lanes] = xt[st, q]
+
+    def quad_in(st):
+        for i in range(1, Q):
+            lanes = pl.ds(pl.multiple_of(wide * ((q + Q - i) % Q), wide), wide)
+            arrive(xq.at[st, :, :, lanes], r_q.at[st * Q + i])
 
     def history(st, s, j):
         base = (st * J + j) * 8
@@ -181,6 +181,8 @@
     into = [
         pltpu.make_async_copy(lesser, x.at[0, pl.ds(0, 2)], s_in.at[1]),
         pltpu.make_async_copy(greater, x.at[0, pl.ds(2, 2)], s_in.at[2]),
+        pltpu.make_async_copy(hopping, hm, s_in.at[3]),
+        pltpu.make_async_copy(coupling, cv, s_in.at[4]),
     ]
     for copy in into:
         copy.start()
@@ -203,12 +205,22 @@
     col = lax.broadcasted_iota(jnp.int32, (ORB + cols, cols), 1)
     when = jnp.where(row < 0, Q * J, ((row >> 5) & 3) * J + (row >> 7))
     pre[...] = jnp.where(jnp.logical_and((row & 31) == (col & 31), (col >> 5) < when), 1.0, 0.0).astype(BF16)
-    one_hot = (
-        lax.broadcasted_iota(jnp.int32, (J * ORB, cols), 1)
-        == lax.broadcasted_iota(jnp.int32, (J * ORB, cols), 0) + J * ORB * q
-    ).astype(F32).astype(BF16)
+    eye[...] = jnp.where(
+        lax.broadcasted_iota(jnp.int32, (cols, cols), 0) == lax.broadcasted_iota(jnp.int32, (cols, cols), 1), 1.0, 0.0
+    ).astype(BF16)
+    from_q = lax.broadcasted_iota(jnp.int32, (Q * wide, cols), 0)
+    to_q = lax.broadcasted_iota(jnp.int32, (Q * wide, cols), 1)
+    packed = (from_q >> 7) * (J * ORB) + (from_q & 127)
+    gather[...] = jnp.where(jnp.logical_and((from_q & 127) < J * ORB, packed == to_q), 1.0, 0.0).astype(BF16)
+    xt[...] = jnp.zeros_like(xt)
     for copy in into:
         copy.wait()
+    across = jnp.broadcast_to(cv[...], (ORB, ORB))
+    same = lax.broadcasted_iota(jnp.int32, (ORB, ORB), 0) == lax.broadcasted_iota(jnp.int32, (ORB, ORB), 1)
+    tall = jnp.sum(jnp.where(same, across, 0.0), axis=1, keepdims=True)
+    same = lax.broadcasted_iota(jnp.int32, (ORB, cols), 0) == (lax.broadcasted_iota(jnp.int32, (ORB, cols), 1) & 31)
+    flat = jnp.sum(jnp.where(same, jnp.broadcast_to(tall, (ORB, cols)), 0.0), axis=0, keepdims=True)
+    w[...] = tall * flat
     hb[0, z] = x[0]
 
     greeted = 2 * (N - 1) + Q - 1
@@ -221,32 +233,40 @@
     def _():
         pl.semaphore_wait(barrier, greeted + 2 * N - 3)
 
-    for j in range(J):
-        mirror_out(0, j)
+    def build(st, zz):
+        got = hb[st, zz]
+        rows = pl.ds(pl.multiple_of(wide * zz, wide), wide)
+        for j in range(J):
+            lr, li, gr, gi = got[0, j], got[1, j], got[2, j], got[3, j]
+            bm[j, rows, 0:cols] = jnp.concatenate([lr, -li, -gr, gi], axis=0)
+            bm[j, rows, cols:2 * cols] = jnp.concatenate([li, lr, -gi, -gr], axis=0)
+        before[...] += jnp.where(zz < z, jnp.sum(got.astype(F32), axis=1), 0.0)
+
+    mirror_out(0, 0)
     history(0, 0, 0)
     history(0, 0, 1)
-    for j in range(J):
-        quad_out(0, j)
+    quad_out(0)
+    mirror_out(0, 1)
+    mirror_out(0, 2)
 
     for st in range(STEPS):
+        earlier, drains[:] = list(drains), []
+        before[...] = jnp.zeros_like(before)
         mirror_on(st, 0)
         if st == 0:
             history(st, 0, 2)
         mirror_on(st, 1)
         mirror_on(st, 2)
         history(st, 1, 0)
-        for j in range(J):
-            quad_on(st, j)
         history(st, 1, 1)
-        for j in range(J):
-            quad_in(st, j)
-        base = [dot(one_hot, xq[st, c].reshape(cols, cols), NT) for c in range(4)]
+        quad_in(st)
+        base = [dot(xq[st, c], gather[...]) for c in range(4)]
 
         for j in range(J):
             mirror_in(st, j)
             part = slice(j * ORB, (j + 1) * ORB)
             mir = f[st, j].reshape(4, ORB, cols).astype(F32)
-            weight = w[part, :]
+            weight = w[...]
 
             def energy(br, bi, mr, mi):
                 sr = br * br - bi * bi
@@ -270,10 +290,14 @@
                 z + i < N, zs_s.at[st], zs_r.at[st, z], s_zs.at[st * N + i], r_zs.at[st * N + i], at((z + i) % N, q, b)
             )
 
+        earlier, drains[:] = earlier + drains, []
         history(st, 1, 2)
+        build(st, z)
         give_partner(st, 0)
         give_far(st, 0)
         history(st, 2, 0)
+        build(st, (z + 1) % N)
+        build(st, (z + N - 1) % N)
         give_partner(st, 1)
         give_far(st, 1)
         history(st, 2, 1)
@@ -295,30 +319,27 @@
         for piece in (2, 3, 4):
             give_partner(st, piece)
             give_far(st, piece)
+        build(st, (z + 2) % N)
+        build(st, (z + N - 2) % N)
         history(st, 3, 0)
         give_far_partner(st, 1)
         history(st, 3, 1)
         history(st, 3, 2)
         for piece in (2, 3, 4):
             give_far_partner(st, piece)
+        build(st, (z + 3) % N)
+        build(st, (z + N - 3) % N)
+        drain_now(earlier)
         for j in range(J):
             history(st, 4, j)
-
-        def build(zz, before):
-            got = hb[st, zz]
-            for j in range(J):
-                lr, li, gr, gi = got[0, j], got[1, j], got[2, j], got[3, j]
-                rows = pl.ds(pl.multiple_of(wide * zz, wide), wide)
-                bm[j, rows, 0:cols] = jnp.concatenate([lr, -li, -gr, gi], axis=0)
-                bm[j, rows, cols:2 * cols] = jnp.concatenate([li, lr, -gi, -gr], axis=0)
-            total = jnp.sum(got.astype(F32), axis=1)
-            return before + jnp.where(zz < z, total, 0.0)
-
-        before = lax.fori_loop(0, N, build, jnp.zeros((4, ORB, cols), F32))
-        ax_s[st] = before.astype(BF16)
+        build(st, (z + 4) % N)
+
+        ax_s[st, 0] = before[...].astype(BF16)
+        ax_s[st, 1] = (before[...] + jnp.sum(x[st].astype(F32), axis=1)).astype(BF16)
         for i in range(1, Q):
             k = st * Q + i
-            push(ax_s.at[st], ax_r.at[st, q], s_ax.at[k], r_ax.at[k], at(z, (q + i) % Q, b))
+            to = (q + i) % Q
+            push(ax_s.at[st, jnp.where(to > q, 1, 0)], ax_r.at[st, q], s_ax.at[k], r_ax.at[k], at(z, to, b))
         if st == 0:
             @pl.when(q == 0)
             def _():
@@ -326,23 +347,6 @@
 
             for i in range(1, Q):
                 push_if(q == 0, hb.at[0, 0, :, 0], ed, s_ed.at[i], r_ed.at[0], at(z, i, b))
-
-        for qq in range(Q - 1):
-            total = jnp.sum(xq[st, :, qq].astype(F32), axis=1)
-            before = before + jnp.where(qq < q, total, 0.0)
-        for i in range(1, Q):
-            arrive(ax_r.at[st, (q + Q - i) % Q], r_ax.at[st * Q + i])
-            before = before + ax_r[st, (q + Q - i) % Q].astype(F32)
-        for c in range(4):
-            level = before[c]
-            levels = [level]
-            for j in range(J - 1):
-                level = level + x[st, c, j].astype(F32)
-                levels.append(level)
-            level = jnp.concatenate(levels, axis=0)
-            high = level.astype(BF16)
-            low = (level - high.astype(F32)).astype(BF16)
-            hop[c] = dot(h3[...], high) + dot(h3[...], low)
 
         for i in range(1, N):
             arrive(cs.at[st, (b + N - i) % N], r_cs.at[st * N + i])
@@ -369,10 +373,26 @@
                 k = (st * J + m) * Q + i
                 push(rs_s.at[st, m, to], rs_r.at[st, m, q], s_rs.at[k], r_rs.at[k], at(z, to, b))
 
+        level = before[...]
+        for i in range(1, Q):
+            arrive(ax_r.at[st, (q + Q - i) % Q], r_ax.at[st * Q + i])
+            level = level + ax_r[st, (q + Q - i) % Q].astype(F32)
+        for c in range(4):
+            run = level[c]
+            runs = [run]
+            for j in range(J - 1):
+                run = run + x[st, c, j].astype(F32)
+                runs.append(run)
+            run = jnp.concatenate(runs, axis=1)
+            high = run.astype(BF16)
+            low = (run - high.astype(F32)).astype(BF16)
+            hop[c] = dot(hm[...], high) + dot(hm[...], low)
         if st == 0:
             @pl.when(q != 0)
             def _():
                 arrive(ed, r_ed.at[0])
+        earlier, drains[:] = list(drains), []
+        drain_now(earlier)
 
         for m in range(J):
             coll = acc[pl.ds(pl.multiple_of(ORB + m * wide + ORB * q, ORB), ORB), :]
@@ -382,74 +402,79 @@
             coll = dt * coll
             for c in range(4):
                 edge = ed[c].astype(F32)
+                lanes = slice(m * cols, (m + 1) * cols)
                 if c % 2 == 0:
-                    new = edge + dt * (hop[c + 1, m * ORB:(m + 1) * ORB] + coll[:, cols:])
+                    new = edge + dt * (hop[c + 1, :, lanes] + coll[:, cols:])
                 else:
-                    new = edge - dt * (hop[c - 1, m * ORB:(m + 1) * ORB] + coll[:, :cols])
-                new = new.astype(BF16)
+                    new = edge - dt * (hop[c - 1, :, lanes] + coll[:, :cols])
                 if st + 1 < STEPS:
-                    x[st + 1, c, m] = new
-                elif c < 2:
-                    out_l[c, m] = new
+                    x[st + 1, c, m] = new.astype(BF16)
                 else:
-                    out_g[c - 2, m] = new
+                    out[c, m] = new.astype(BF16)
             if st + 1 < STEPS:
                 hb[st + 1, z, :, m] = x[st + 1, :, m]
                 mirror_out(st + 1, m)
-                quad_out(st + 1, m)
                 history(st + 1, 0, m)
-
-    for drain in drains:
-        drain()
+        if st + 1 < STEPS:
+            quad_out(st + 1)
+
+    drain_now(drains)
 
 
 def per_device(lesser, greater, hopping, coupling):
     rows, cols = lesser.shape[1:]
     dt = 3.0 / (rows * N * Q // ORB)
-    w = jnp.tile(coupling, rows // ORB)[:, None] * jnp.tile(coupling, cols // ORB)[None, :]
-    h3 = jnp.kron(jnp.eye(rows // ORB, dtype=hopping.dtype), hopping)
-    part = (2, J, ORB, cols)
     wide = 4 * ORB
 
     def dma(n):
         return pltpu.SemaphoreType.DMA((n,))
 
-    one = [dma(3)]
-    pairs = [STEPS * J * N, STEPS * J * N, STEPS * J * 3, STEPS * J * 8, STEPS * len(PIECES) * 7]
+    sems = [dma(5)]
+    pairs = [STEPS * J * N, STEPS * J * N, STEPS * Q, STEPS * J * 8, STEPS * len(PIECES) * 7]
     pairs += [STEPS * N, STEPS * N, STEPS * J * Q, STEPS * Q, Q]
     for n in pairs:
-        one += [dma(n), dma(n)]
-    outs = pl.pallas_call(
+        sems += [dma(n), dma(n)]
+    buffers = [
+        ((STEPS, 4, J, ORB, cols), BF16),
+        ((STEPS, Q, 4, J * ORB, wide), BF16),
+        ((STEPS, 4, J * ORB, Q * wide), BF16),
+        ((STEPS, J, N, HALF, cols), BF16),
+        ((STEPS, J, N, HALF, cols), BF16),
+        ((STEPS, J, ORB + cols, N * wide), BF16),
+        ((STEPS, N, 4, J, ORB, cols), BF16),
+        ((J, N * wide, 2 * cols), BF16),
+        ((ORB + cols, 2 * cols), F32),
+        ((ORB + cols, cols), BF16),
+        ((cols, cols), BF16),
+        ((Q * wide, cols), BF16),
+        ((ORB, cols), F32),
+        ((ORB, ORB), BF16),
+        ((1, ORB), F32),
+        ((4, ORB, cols), F32),
+        ((4, ORB, J * cols), F32),
+        ((STEPS, ORB, cols), BF16),
+        ((STEPS, N, ORB, cols), BF16),
+        ((STEPS, N, ORB, cols), BF16),
+        ((STEPS, J, Q, ORB, 2 * cols), BF16),
+        ((STEPS, J, Q, ORB, 2 * cols), BF16),
+        ((STEPS, 2, 4, ORB, cols), BF16),
+        ((STEPS, Q, 4, ORB, cols), BF16),
+        ((4, ORB, cols), BF16),
+    ]
+    part = (2, J, ORB, cols)
+    new = pl.pallas_call(
         functools.partial(kernel, dt),
-        out_shape=[jax.ShapeDtypeStruct(part, BF16)] * 2,
-        in_specs=[pl.BlockSpec(memory_space=pl.ANY)] * 2 + [pl.BlockSpec(memory_space=pltpu.VMEM)] * 2,
-        out_specs=[pl.BlockSpec(memory_space=pltpu.VMEM)] * 2,
-        scratch_shapes=[
-            pltpu.VMEM((STEPS, 4, J, ORB, cols), BF16),
-            pltpu.VMEM((STEPS, 4, Q, J, ORB, cols), BF16),
-            pltpu.VMEM((STEPS, J, N, HALF, cols), BF16),
-            pltpu.VMEM((STEPS, J, N, HALF, cols), BF16),
-            pltpu.VMEM((STEPS, J, ORB + cols, N * wide), BF16),
-            pltpu.VMEM((STEPS, N, 4, J, ORB, cols), BF16),
-            pltpu.VMEM((J, N * wide, 2 * cols), BF16),
-            pltpu.VMEM((ORB + cols, 2 * cols), F32),
-            pltpu.VMEM((ORB + cols, cols), BF16),
-            pltpu.VMEM((4, J * ORB, cols), F32),
-            pltpu.VMEM((STEPS, ORB, cols), BF16),
-            pltpu.VMEM((STEPS, N, ORB, cols), BF16),
-            pltpu.VMEM((STEPS, N, ORB, cols), BF16),
-            pltpu.VMEM((STEPS, J, Q, ORB, 2 * cols), BF16),
-            pltpu.VMEM((STEPS, J, Q, ORB, 2 * cols), BF16),
-            pltpu.VMEM((STEPS, 4, ORB, cols), BF16),
-            pltpu.VMEM((STEPS, Q, 4, ORB, cols), BF16),
-            pltpu.VMEM((4, ORB, cols), BF16),
-        ] + one,
+        out_shape=jax.ShapeDtypeStruct((4, J, ORB, cols), BF16),
+        in_specs=[pl.BlockSpec(memory_space=pl.ANY)] * 4,
+        out_specs=pl.BlockSpec(memory_space=pltpu.VMEM),
+        scratch_shapes=[pltpu.VMEM(shape, dtype) for shape, dtype in buffers] + sems,
         compiler_params=pltpu.CompilerParams(
             collective_id=0, has_side_effects=True, vmem_limit_bytes=56 * 1024 * 1024
         ),
         cost_estimate=pl.CostEstimate(flops=4 * 10**9, bytes_accessed=10**6, transcendentals=0),
-    )(lesser.reshape(part), greater.reshape(part), w, h3)
-    return outs[0].reshape(lesser.shape), outs[1].reshape(greater.shape)
+    )(lesser.reshape(part), greater.reshape(part), hopping, coupling.reshape(1, ORB))
+    new = new.reshape(4, rows, cols)
+    return new[:2], new[2:]
 
 
 def solution(mesh):

time: 129 us -> 114 us (0.88)
  Pallas kernels: 123 us -> 112 us
  local copies, waits for them, and re-layouts: 4.43 us -> 1.72 us
    pallas_call x1, Pallas kernels: 123 us -> 112 us  [per_device(): pl.pallas_call(functools.partial(kernel, dt), out_shape=jax.ShapeDtypeStr...]
    unnamed x8 -> x0, local copies, waits for them, and re-layouts: 3.54 us -> none
    slice x0 -> x1, local copies, waits for them, and re-layouts: none -> 1.72 us  [per_device(): return (new[:2], new[2:])]
where the time goes in v3:
time: 114 us
  Pallas kernels  112 us (98%)
  local copies, waits for them, and re-layouts  1.72 us (2%)
    pallas_call x1, Pallas kernels, per_device(): pl.pallas_call(functools.partial(kernel, dt), out_shape=jax.ShapeDtypeStr...  112 us

profile of v3, /device:TPU:1, one launch (start us, length us, event | category | flops | bytes accessed | tf_op | source)
XLA Modules:
  0.0 114.0 jit_solution(4846767098962148575)
XLA Ops:
  0.6 111.7 %shard_map.59 = bf16[4,3,32,384]{3,2,1,0:T(8,128)(2,1)} custom-call(bf16[2,3,32,384]{3,2,1,0:T(8,128)(2,1)} %bitcast.7, bf16[2,3,32,384]{3,2,1,0:T(8,128)(2,1)} %bitcast.8, bf16[32,32]{1,0:T(8,128)(2,1)} %hopping.1, f32[1,32]{1,0:T(1,128)} %bitcast.9), custom_call_target="tpu_custom_call" | custom-call | flops 4000000000 | bytes 1000000 | tf_op jit(solution)/shard_map/pallas_call | solution.py:465
  112.3 1.7 %fusion = (bf16[2,3,32,384]{3,2,1,0:T(8,128)(2,1)}, bf16[2,3,32,384]{3,2,1,0:T(8,128)(2,1)}) fusion(bf16[4,3,32,384]{3,2,1,0:T(8,128)(2,1)} %shard_map.59), kind=kLoop, calls=%fused_computation | loop fusion | bytes 589824 | tf_op jit(solution)/shard_map/slice | solution.py:477

commit v4 on v3

--- a/solution.py
+++ b/solution.py
@@ -54,24 +54,13 @@
         )
 
     def push(src, dst, ss, rs, where):
-        copy = copy_of(src, dst, ss, rs, where)
-        copy.start()
-        drains.append(copy.wait_send)
-
-    def push_if(cond, src, dst, ss, rs, where):
-        @pl.when(cond)
-        def _():
-            copy_of(src, dst, ss, rs, where).start()
-
-        def drain():
-            @pl.when(cond)
-            def _():
-                copy_of(src, dst, ss, rs, where).wait_send()
-
-        drains.append(drain)
-
-    def arrive(dst, rs):
-        copy_of(dst, dst, s_in.at[0], rs, at(z, q, b)).wait_recv()
+        copy_of(src, dst, ss, rs, where).start()
+
+    def owe(ref, ss):
+        drains.append(copy_of(ref, ref, ss, s_in.at[0], at(z, q, b)).wait_send)
+
+    def arrive(ref, rs):
+        copy_of(ref, ref, s_in.at[0], rs, at(z, q, b)).wait_recv()
 
     def place(dx, dy):
         return ((xh + dx) % 2) * Y + (y + dy) % Y
@@ -80,78 +69,90 @@
 
 
     def mirror_out(st, j):
+        k = st * J + j
         for i in range(1, N):
             p = (b + i) % N
-            k = (st * J + j) * N + i
             src = x.at[st, p // 2, j, pl.ds(pl.multiple_of(HALF * (p % 2), HALF), HALF)]
             push(src, t1.at[st, j, b], s_t1.at[k], r_t1.at[k], at(z, q, p))
+        owe(t1.at[st, j, pl.ds(0, N - 1)], s_t1.at[k])
         t1[st, j, b] = x[st, b // 2, j, pl.ds(pl.multiple_of(HALF * (b % 2), HALF), HALF)]
 
     def mirror_on(st, j):
-        base = (st * J + j) * N
+        k = st * J + j
+        arrive(t1.at[st, j, pl.ds(0, N - 1)], r_t1.at[k])
         for i in range(N):
             bb = (b + N - i) % N
-            if i > 0:
-                arrive(t1.at[st, j, bb], r_t1.at[base + i])
             here = jnp.logical_and(bb == z, b == z)
-            push_if(
-                jnp.logical_not(here), t1.at[st, j, bb], f.at[st, j, b], s_t2.at[base + i], r_t2.at[base + b], at(bb, q, z)
-            )
+
+            @pl.when(jnp.logical_not(here))
+            def _():
+                push(t1.at[st, j, bb], f.at[st, j, b], s_t2.at[k], r_t2.at[k], at(bb, q, z))
 
             @pl.when(here)
             def _():
                 f[st, j, b] = t1[st, j, bb]
 
+        def drain():
+            for n, cond in ((N - 1, b == z), (N, b != z)):
+                @pl.when(cond)
+                def _():
+                    ref = t1.at[st, j, pl.ds(0, n)]
+                    copy_of(ref, ref, s_t2.at[k], s_in.at[0], at(z, q, b)).wait_send()
+
+        drains.append(drain)
+
     def mirror_in(st, j):
-        base = (st * J + j) * N
-        for i in range(N):
-            p = (b + i) % N
-            if i > 0:
-                arrive(f.at[st, j, p], r_t2.at[base + p])
-            else:
-                @pl.when(b != z)
-                def _():
-                    arrive(f.at[st, j, p], r_t2.at[base + p])
+        for n, cond in ((N - 1, b == z), (N, b != z)):
+            @pl.when(cond)
+            def _():
+                arrive(f.at[st, j, pl.ds(0, n)], r_t2.at[st * J + j])
 
     def quad_out(st):
         for c in range(4):
             xt[st, :, c, :, 0:J * ORB] = dot(eye[...], x[st, c].reshape(J * ORB, cols), NT).astype(BF16).reshape(Q, J * ORB, J * ORB)
         lanes = pl.ds(pl.multiple_of(wide * q, wide), wide)
-        for i in range(1, Q):
-            k = st * Q + i
-            to = (q + i) % Q
-            push(xt.at[st, to], xq.at[st, :, :, lanes], s_q.at[k], r_q.at[k], at(z, to, b))
+        for j in range(J):
+            part = pl.ds(j * ORB, ORB)
+            k = st * J + j
+            for i in range(1, Q):
+                to = (q + i) % Q
+                push(xt.at[st, to, :, part], xq.at[st, :, part, lanes], s_q.at[k], r_q.at[k], at(z, to, b))
+            owe(xq.at[st, :, part, pl.ds(0, (Q - 1) * wide)], s_q.at[k])
         xq[st, :, :, lanes] = xt[st, q]
 
-    def quad_in(st):
-        for i in range(1, Q):
-            lanes = pl.ds(pl.multiple_of(wide * ((q + Q - i) % Q), wide), wide)
-            arrive(xq.at[st, :, :, lanes], r_q.at[st * Q + i])
+    def quad_in(st, j):
+        arrive(xq.at[st, :, pl.ds(j * ORB, ORB), pl.ds(0, (Q - 1) * wide)], r_q.at[st * J + j])
 
     def history(st, s, j):
-        base = (st * J + j) * 8
+        k = st * J + j
         lo, hi = (z + N - s) % N, (z + s) % N
-        first, second = (pl.ds(0, 2), pl.ds(2, 2)) if s >= 3 else (pl.ds(0, 4), pl.ds(0, 4))
         if s > 0:
-            got = (pl.ds(0, 2), pl.ds(2, 2)) if s == 4 else (pl.ds(0, 4), pl.ds(0, 4))
-            arrive(hb.at[st, lo, got[0], j], r_h.at[base + 2 * s - 2])
-            arrive(hb.at[st, hi, got[1], j], r_h.at[base + 2 * s - 1])
+            arrive(hb.at[st, pl.ds(0, 1 if s == 4 else 2), :, j], r_h.at[4 * k + s - 1])
         if s < 4:
+            first, second = (pl.ds(0, 2), pl.ds(2, 2)) if s == 3 else (pl.ds(0, 4), pl.ds(0, 4))
             one, two = hb.at[st, lo, first, j], hb.at[st, hi, second, j]
             from_one, from_two = (x.at[st, :, j], x.at[st, :, j]) if s == 0 else (one, two)
-            push(from_one, one, s_h.at[base + 2 * s], r_h.at[base + 2 * s], up)
-            push(from_two, two, s_h.at[base + 2 * s + 1], r_h.at[base + 2 * s + 1], down)
+            push(from_one, one, s_h.at[k], r_h.at[4 * k + s], up)
+            push(from_two, two, s_h.at[k], r_h.at[4 * k + s], down)
+        if s == 3:
+            owe(hb.at[st, pl.ds(0, N - 1), :, j], s_h.at[k])
 
     def tile(st, piece, bb):
         k, m, n = PIECES[piece]
         return sg.at[st, k, pl.ds(ORB * (1 + m), ORB * n), pl.ds(pl.multiple_of(wide * bb, wide), wide)]
 
+    WAIT = (0, 1, 3, 3, 2, 3, 3)
+
+    def several(st, piece, n):
+        k, m, rows = PIECES[piece]
+        return sg.at[st, k, pl.ds(ORB * (1 + m), ORB * rows), pl.ds(0, n * wide)]
+
     def give(st, piece, way, bb, to):
-        k = (st * len(PIECES) + piece) * 7 + way
-        push(tile(st, piece, bb), tile(st, piece, bb), s_g.at[k], r_g.at[k], at(z, q, to))
-
-    def take(st, piece, way, bb):
-        arrive(tile(st, piece, bb), r_g.at[(st * len(PIECES) + piece) * 7 + way])
+        k = st * len(PIECES) + piece
+        push(tile(st, piece, bb), tile(st, piece, bb), s_g.at[k], r_g.at[4 * k + WAIT[way]], at(z, q, to))
+
+    def take(st, piece, wait):
+        arrive(several(st, piece, 4 if wait == 3 else 1), r_g.at[4 * (st * len(PIECES) + piece) + wait])
 
     def give_own(st, piece):
         give(st, piece, 0, b, place(1, 0))
@@ -159,23 +160,21 @@
         give(st, piece, 2, b, place(0, 3))
 
     def give_partner(st, piece):
-        take(st, piece, 0, place(1, 0))
+        take(st, piece, 0)
         give(st, piece, 3, place(1, 0), place(0, 1))
         give(st, piece, 4, place(1, 0), place(0, 3))
 
     def give_far(st, piece):
-        take(st, piece, 1, place(0, 3))
+        take(st, piece, 1)
         give(st, piece, 5, place(0, 3), place(0, 1))
 
     def give_far_partner(st, piece):
-        take(st, piece, 4, place(1, 1))
+        take(st, piece, 2)
         give(st, piece, 6, place(1, 1), place(0, 3))
+        owe(several(st, piece, 7), s_g.at[st * len(PIECES) + piece])
 
     def take_rest(st, piece):
-        take(st, piece, 2, place(0, 1))
-        take(st, piece, 3, place(1, 3))
-        take(st, piece, 5, place(0, 2))
-        take(st, piece, 6, place(1, 2))
+        take(st, piece, 3)
 
 
     into = [
@@ -192,15 +191,6 @@
         pl.semaphore_signal(barrier, inc=1, device_id=at(z, q, (b + i) % N), device_id_type=MESH)
     for i in range(1, Q):
         pl.semaphore_signal(barrier, inc=1, device_id=at(z, (q + i) % Q, b), device_id_type=MESH)
-    for i in range(N):
-        bb = (b + i) % N
-
-        @pl.when(jnp.logical_and(bb != z, b != z))
-        def _():
-            pl.semaphore_signal(barrier, inc=1, device_id=at(bb, q, z), device_id_type=MESH)
-            if i > 0:
-                pl.semaphore_signal(barrier, inc=1, device_id=at(b, q, bb), device_id_type=MESH)
-
     row = lax.broadcasted_iota(jnp.int32, (ORB + cols, cols), 0) - ORB
     col = lax.broadcasted_iota(jnp.int32, (ORB + cols, cols), 1)
     when = jnp.where(row < 0, Q * J, ((row >> 5) & 3) * J + (row >> 7))
@@ -221,17 +211,10 @@
     same = lax.broadcasted_iota(jnp.int32, (ORB, cols), 0) == (lax.broadcasted_iota(jnp.int32, (ORB, cols), 1) & 31)
     flat = jnp.sum(jnp.where(same, jnp.broadcast_to(tall, (ORB, cols)), 0.0), axis=0, keepdims=True)
     w[...] = tall * flat
+
     hb[0, z] = x[0]
 
-    greeted = 2 * (N - 1) + Q - 1
-
-    @pl.when(b == z)
-    def _():
-        pl.semaphore_wait(barrier, greeted)
-
-    @pl.when(b != z)
-    def _():
-        pl.semaphore_wait(barrier, greeted + 2 * N - 3)
+    pl.semaphore_wait(barrier, 2 * (N - 1) + Q - 1)
 
     def build(st, zz):
         got = hb[st, zz]
@@ -245,6 +228,7 @@
     mirror_out(0, 0)
     history(0, 0, 0)
     history(0, 0, 1)
+
     quad_out(0)
     mirror_out(0, 1)
     mirror_out(0, 2)
@@ -258,13 +242,11 @@
         mirror_on(st, 1)
         mirror_on(st, 2)
         history(st, 1, 0)
-        history(st, 1, 1)
-        quad_in(st)
-        base = [dot(xq[st, c], gather[...]) for c in range(4)]
 
         for j in range(J):
+            quad_in(st, j)
+            base = [dot(xq[st, c, j * ORB:(j + 1) * ORB], gather[...]) for c in range(4)]
             mirror_in(st, j)
-            part = slice(j * ORB, (j + 1) * ORB)
             mir = f[st, j].reshape(4, ORB, cols).astype(F32)
             weight = w[...]
 
@@ -274,8 +256,7 @@
                 return [((sr * mr - si * mi) * weight).astype(BF16), ((sr * mi + si * mr) * weight).astype(BF16)]
 
             sigma = jnp.concatenate(
-                energy(base[2][part], base[3][part], mir[0], mir[1])
-                + energy(base[0][part], base[1][part], mir[2], mir[3]),
+                energy(base[2], base[3], mir[0], mir[1]) + energy(base[0], base[1], mir[2], mir[3]),
                 axis=0,
             )
             summed = dot(pre[...], sigma, NT).astype(BF16)
@@ -284,46 +265,45 @@
             for piece, (k, _, _) in enumerate(PIECES):
                 if k == j:
                     give_own(st, piece)
+            if j < 2:
+                history(st, 1, 1 + j)
 
         for i in range(1, N):
-            push_if(
-                z + i < N, zs_s.at[st], zs_r.at[st, z], s_zs.at[st * N + i], r_zs.at[st * N + i], at((z + i) % N, q, b)
-            )
+            push(zs_s.at[st], zs_r.at[st, z], s_zs.at[st], r_zs.at[st], at((z + i) % N, q, b))
+        owe(zs_r.at[st, pl.ds(0, N - 1)], s_zs.at[st])
 
         earlier, drains[:] = earlier + drains, []
-        history(st, 1, 2)
+        history(st, 2, 0)
         build(st, z)
         give_partner(st, 0)
         give_far(st, 0)
-        history(st, 2, 0)
+        history(st, 2, 1)
         build(st, (z + 1) % N)
         build(st, (z + N - 1) % N)
         give_partner(st, 1)
         give_far(st, 1)
-        history(st, 2, 1)
+        history(st, 2, 2)
 
         carry = jnp.zeros((ORB, cols), F32)
-        for i in range(1, N):
-            @pl.when(z - i >= 0)
-            def _():
-                arrive(zs_r.at[st, (z + N - i) % N], r_zs.at[st * N + i])
+        arrive(zs_r.at[st, pl.ds(0, N - 1)], r_zs.at[st])
         for zz in range(N - 1):
             carry = carry + jnp.where(zz < z, zs_r[st, zz].astype(F32), 0.0)
         cs[st, b] = carry.astype(BF16)
         for i in range(1, N):
-            k = st * N + i
-            push(cs.at[st, b], cs.at[st, b], s_cs.at[k], r_cs.at[k], at(z, q, (b + i) % N))
+            push(cs.at[st, b], cs.at[st, b], s_cs.at[st], r_cs.at[st], at(z, q, (b + i) % N))
+        owe(cs.at[st, pl.ds(0, N - 1)], s_cs.at[st])
 
         give_far_partner(st, 0)
-        history(st, 2, 2)
-        for piece in (2, 3, 4):
+        history(st, 3, 0)
+        give_partner(st, 2)
+        give_far(st, 2)
+        give_far_partner(st, 1)
+        history(st, 3, 1)
+        build(st, (z + 2) % N)
+        build(st, (z + N - 2) % N)
+        for piece in (3, 4):
             give_partner(st, piece)
             give_far(st, piece)
-        build(st, (z + 2) % N)
-        build(st, (z + N - 2) % N)
-        history(st, 3, 0)
-        give_far_partner(st, 1)
-        history(st, 3, 1)
         history(st, 3, 2)
         for piece in (2, 3, 4):
             give_far_partner(st, piece)
@@ -336,20 +316,20 @@
 
         ax_s[st, 0] = before[...].astype(BF16)
         ax_s[st, 1] = (before[...] + jnp.sum(x[st].astype(F32), axis=1)).astype(BF16)
-        for i in range(1, Q):
-            k = st * Q + i
-            to = (q + i) % Q
-            push(ax_s.at[st, jnp.where(to > q, 1, 0)], ax_r.at[st, q], s_ax.at[k], r_ax.at[k], at(z, to, b))
+        sib = (q // 2) * 2 + (1 - q % 2)
+        par = (q + 2) % Q
+        dia = (sib + 2) % Q
+        k = st * 3
+        push(ax_s.at[st, 1 - q // 2], ax_r.at[st, q], s_ax.at[st], r_ax.at[k], at(z, par, b))
+        push(ax_s.at[st, 1 - q % 2], ax_r.at[st, q], s_ax.at[st], r_ax.at[k + 1], at(z, sib, b))
         if st == 0:
             @pl.when(q == 0)
             def _():
                 ed[...] = hb[0, 0, :, 0]
-
-            for i in range(1, Q):
-                push_if(q == 0, hb.at[0, 0, :, 0], ed, s_ed.at[i], r_ed.at[0], at(z, i, b))
-
-        for i in range(1, N):
-            arrive(cs.at[st, (b + N - i) % N], r_cs.at[st * N + i])
+                for i in range(1, Q):
+                    push(hb.at[0, 0, :, 0], ed, s_ed.at[0], r_ed.at[0], at(z, i, b))
+
+        arrive(cs.at[st, pl.ds(0, N - 1)], r_cs.at[st])
         for bb in range(N):
             for j in range(J):
                 sg[st, j, 0:ORB, bb * wide:(bb + 1) * wide] = cs[st, bb, :, j * wide:(j + 1) * wide]
@@ -357,6 +337,17 @@
         acc[...] = dot(sg[st, 0], bm[0])
         take_rest(st, 1)
         acc[...] += dot(sg[st, 1], bm[1])
+
+        def rows_of(m, qq):
+            return acc[pl.ds(pl.multiple_of(ORB + m * wide + ORB * qq, ORB), ORB), :]
+
+        def cross(m):
+            k = 2 * (st * J + m)
+            arrive(rs_r.at[st, m, pl.ds(0, 2)], r_rs.at[k])
+            rs_s[st, m, 2] = (rows_of(m, par) + rs_r[st, m, 1].astype(F32)).astype(BF16)
+            push(rs_s.at[st, m, 2], rs_r.at[st, m, 2], s_rs.at[k + 1], r_rs.at[k + 1], at(z, par, b))
+            owe(rs_s.at[st, m, 2], s_rs.at[k + 1])
+
         lead = None
         for m in range(J):
             take_rest(st, 2 + m)
@@ -367,16 +358,24 @@
                 part = part[ORB:]
             part = part + lead
             acc[ORB + m * wide:hi, :] = part
-            rs_s[st, m] = part.reshape(Q, ORB, 2 * cols).astype(BF16)
-            for i in range(1, Q):
-                to = (q + i) % Q
-                k = (st * J + m) * Q + i
-                push(rs_s.at[st, m, to], rs_r.at[st, m, q], s_rs.at[k], r_rs.at[k], at(z, to, b))
+            rs_s[st, m, 0] = rows_of(m, sib).astype(BF16)
+            rs_s[st, m, 1] = rows_of(m, dia).astype(BF16)
+            k = 2 * (st * J + m)
+            push(rs_s.at[st, m, pl.ds(0, 2)], rs_r.at[st, m, pl.ds(0, 2)], s_rs.at[k], r_rs.at[k], at(z, sib, b))
+            owe(rs_s.at[st, m, pl.ds(0, 2)], s_rs.at[k])
+            if m > 0:
+                cross(m - 1)
+        cross(J - 1)
 
         level = before[...]
-        for i in range(1, Q):
-            arrive(ax_r.at[st, (q + Q - i) % Q], r_ax.at[st * Q + i])
-            level = level + ax_r[st, (q + Q - i) % Q].astype(F32)
+        k = st * 3
+        arrive(ax_r.at[st, par], r_ax.at[k])
+        push(ax_r.at[st, par], ax_r.at[st, par], s_ax.at[st], r_ax.at[k + 2], at(z, sib, b))
+        owe(ax_r.at[st, pl.ds(0, 3)], s_ax.at[st])
+        arrive(ax_r.at[st, sib], r_ax.at[k + 1])
+        arrive(ax_r.at[st, dia], r_ax.at[k + 2])
+        for other in (par, sib, dia):
+            level = level + ax_r[st, other].astype(F32)
         for c in range(4):
             run = level[c]
             runs = [run]
@@ -391,14 +390,20 @@
             @pl.when(q != 0)
             def _():
                 arrive(ed, r_ed.at[0])
+
+            def drain():
+                @pl.when(q == 0)
+                def _():
+                    ref = ax_r.at[0, pl.ds(0, 3)]
+                    copy_of(ref, ref, s_ed.at[0], s_in.at[0], at(z, q, b)).wait_send()
+
+            drains.append(drain)
         earlier, drains[:] = list(drains), []
         drain_now(earlier)
 
         for m in range(J):
-            coll = acc[pl.ds(pl.multiple_of(ORB + m * wide + ORB * q, ORB), ORB), :]
-            for i in range(1, Q):
-                arrive(rs_r.at[st, m, (q + Q - i) % Q], r_rs.at[(st * J + m) * Q + i])
-                coll = coll + rs_r[st, m, (q + Q - i) % Q].astype(F32)
+            arrive(rs_r.at[st, m, 2], r_rs.at[2 * (st * J + m) + 1])
+            coll = rows_of(m, q) + rs_r[st, m, 0].astype(F32) + rs_r[st, m, 2].astype(F32)
             coll = dt * coll
             for c in range(4):
                 edge = ed[c].astype(F32)
@@ -429,11 +434,14 @@
     def dma(n):
         return pltpu.SemaphoreType.DMA((n,))
 
+    pieces = STEPS * J
     sems = [dma(5)]
-    pairs = [STEPS * J * N, STEPS * J * N, STEPS * Q, STEPS * J * 8, STEPS * len(PIECES) * 7]
-    pairs += [STEPS * N, STEPS * N, STEPS * J * Q, STEPS * Q, Q]
-    for n in pairs:
-        sems += [dma(n), dma(n)]
+    for sent, got in (
+        (pieces, pieces), (pieces, pieces), (pieces, pieces), (pieces, 4 * pieces),
+        (STEPS * len(PIECES), STEPS * len(PIECES) * 4), (STEPS, STEPS), (STEPS, STEPS),
+        (2 * pieces, 2 * pieces), (STEPS, 3 * STEPS), (1, 1),
+    ):
+        sems += [dma(sent), dma(got)]
     buffers = [
         ((STEPS, 4, J, ORB, cols), BF16),
         ((STEPS, Q, 4, J * ORB, wide), BF16),
@@ -455,8 +463,8 @@
         ((STEPS, ORB, cols), BF16),
         ((STEPS, N, ORB, cols), BF16),
         ((STEPS, N, ORB, cols), BF16),
-        ((STEPS, J, Q, ORB, 2 * cols), BF16),
-        ((STEPS, J, Q, ORB, 2 * cols), BF16),
+        ((STEPS, J, 3, ORB, 2 * cols), BF16),
+        ((STEPS, J, 3, ORB, 2 * cols), BF16),
         ((STEPS, 2, 4, ORB, cols), BF16),
         ((STEPS, Q, 4, ORB, cols), BF16),
         ((4, ORB, cols), BF16),

time: 114 us -> 105 us (0.921)
  Pallas kernels: 112 us -> 103 us
    pallas_call x1, Pallas kernels: 112 us -> 103 us  [per_device(): pl.pallas_call(functools.partial(kernel, dt), out_shape=jax.ShapeDtypeStr...]
where the time goes in v4:
time: 105 us
  Pallas kernels  103 us (98%)
  local copies, waits for them, and re-layouts  1.72 us (2%)
    pallas_call x1, Pallas kernels, per_device(): pl.pallas_call(functools.partial(kernel, dt), out_shape=jax.ShapeDtypeStr...  103 us

profile of v4, /device:TPU:1, one launch (start us, length us, event | category | flops | bytes accessed | tf_op | source)
XLA Modules:
  0.0 105.3 jit_solution(9686293699464672798)
XLA Ops:
  0.6 103.0 %shard_map.59 = bf16[4,3,32,384]{3,2,1,0:T(8,128)(2,1)} custom-call(bf16[2,3,32,384]{3,2,1,0:T(8,128)(2,1)} %bitcast.7, bf16[2,3,32,384]{3,2,1,0:T(8,128)(2,1)} %bitcast.8, bf16[32,32]{1,0:T(8,128)(2,1)} %hopping.1, f32[1,32]{1,0:T(1,128)} %bitcast.9), custom_call_target="tpu_custom_call" | custom-call | flops 4000000000 | bytes 1000000 | tf_op jit(solution)/shard_map/pallas_call | solution.py:473
  103.6 1.7 %fusion = (bf16[2,3,32,384]{3,2,1,0:T(8,128)(2,1)}, bf16[2,3,32,384]{3,2,1,0:T(8,128)(2,1)}) fusion(bf16[4,3,32,384]{3,2,1,0:T(8,128)(2,1)} %shard_map.59), kind=kLoop, calls=%fused_computation | loop fusion | bytes 589824 | tf_op jit(solution)/shard_map/slice | solution.py:485

commit v5 on v4

--- a/solution.py
+++ b/solution.py
@@ -228,20 +228,20 @@
     mirror_out(0, 0)
     history(0, 0, 0)
     history(0, 0, 1)
-
-    quad_out(0)
+    history(0, 0, 2)
+
     mirror_out(0, 1)
     mirror_out(0, 2)
+    quad_out(0)
 
     for st in range(STEPS):
         earlier, drains[:] = list(drains), []
         before[...] = jnp.zeros_like(before)
         mirror_on(st, 0)
-        if st == 0:
-            history(st, 0, 2)
         mirror_on(st, 1)
         mirror_on(st, 2)
         history(st, 1, 0)
+        history(st, 1, 1)
 
         for j in range(J):
             quad_in(st, j)
@@ -265,25 +265,28 @@
             for piece, (k, _, _) in enumerate(PIECES):
                 if k == j:
                     give_own(st, piece)
-            if j < 2:
-                history(st, 1, 1 + j)
+            if j == 0:
+                history(st, 1, 2)
+            if j == 1:
+                history(st, 2, 0)
 
         for i in range(1, N):
             push(zs_s.at[st], zs_r.at[st, z], s_zs.at[st], r_zs.at[st], at((z + i) % N, q, b))
         owe(zs_r.at[st, pl.ds(0, N - 1)], s_zs.at[st])
 
         earlier, drains[:] = earlier + drains, []
-        history(st, 2, 0)
+        history(st, 2, 1)
         build(st, z)
         give_partner(st, 0)
         give_far(st, 0)
-        history(st, 2, 1)
         build(st, (z + 1) % N)
         build(st, (z + N - 1) % N)
         give_partner(st, 1)
         give_far(st, 1)
         history(st, 2, 2)
-
+        give_far_partner(st, 0)
+        give_partner(st, 2)
+        give_far(st, 2)
         carry = jnp.zeros((ORB, cols), F32)
         arrive(zs_r.at[st, pl.ds(0, N - 1)], r_zs.at[st])
         for zz in range(N - 1):
@@ -293,20 +296,19 @@
             push(cs.at[st, b], cs.at[st, b], s_cs.at[st], r_cs.at[st], at(z, q, (b + i) % N))
         owe(cs.at[st, pl.ds(0, N - 1)], s_cs.at[st])
 
-        give_far_partner(st, 0)
         history(st, 3, 0)
-        give_partner(st, 2)
-        give_far(st, 2)
+        give_partner(st, 3)
+        give_far(st, 3)
+        give_partner(st, 4)
+        give_far(st, 4)
         give_far_partner(st, 1)
         history(st, 3, 1)
         build(st, (z + 2) % N)
         build(st, (z + N - 2) % N)
-        for piece in (3, 4):
-            give_partner(st, piece)
-            give_far(st, piece)
         history(st, 3, 2)
-        for piece in (2, 3, 4):
-            give_far_partner(st, piece)
+        give_far_partner(st, 2)
+        give_far_partner(st, 3)
+        give_far_partner(st, 4)
         build(st, (z + 3) % N)
         build(st, (z + N - 3) % N)
         drain_now(earlier)

time: 105 us -> 104 us (level)
    pallas_call x1, Pallas kernels: 103 us -> 102 us  [per_device(): pl.pallas_call(functools.partial(kernel, dt), out_shape=jax.ShapeDtypeStr...]
where the time goes in v5:
time: 104 us
  Pallas kernels  102 us (98%)
  local copies, waits for them, and re-layouts  1.72 us (2%)
    pallas_call x1, Pallas kernels, per_device(): pl.pallas_call(functools.partial(kernel, dt), out_shape=jax.ShapeDtypeStr...  102 us

profile of v5, /device:TPU:1, one launch (start us, length us, event | category | flops | bytes accessed | tf_op | source)
XLA Modules:
  0.0 104.0 jit_solution(18264707567246843771)
XLA Ops:
  0.6 101.6 %shard_map.59 = bf16[4,3,32,384]{3,2,1,0:T(8,128)(2,1)} custom-call(bf16[2,3,32,384]{3,2,1,0:T(8,128)(2,1)} %bitcast.7, bf16[2,3,32,384]{3,2,1,0:T(8,128)(2,1)} %bitcast.8, bf16[32,32]{1,0:T(8,128)(2,1)} %hopping.1, f32[1,32]{1,0:T(1,128)} %bitcast.9), custom_call_target="tpu_custom_call" | custom-call | flops 4000000000 | bytes 1000000 | tf_op jit(solution)/shard_map/pallas_call | solution.py:475
  102.3 1.7 %fusion = (bf16[2,3,32,384]{3,2,1,0:T(8,128)(2,1)}, bf16[2,3,32,384]{3,2,1,0:T(8,128)(2,1)}) fusion(bf16[4,3,32,384]{3,2,1,0:T(8,128)(2,1)} %shard_map.59), kind=kLoop, calls=%fused_computation | loop fusion | bytes 589824 | tf_op jit(solution)/shard_map/slice | solution.py:487

commit v6 on v5

--- a/solution.py
+++ b/solution.py
@@ -350,6 +350,7 @@
             push(rs_s.at[st, m, 2], rs_r.at[st, m, 2], s_rs.at[k + 1], r_rs.at[k + 1], at(z, par, b))
             owe(rs_s.at[st, m, 2], s_rs.at[k + 1])
 
+        settled, drains[:] = list(drains), []
         lead = None
         for m in range(J):
             take_rest(st, 2 + m)
@@ -400,8 +401,7 @@
                     copy_of(ref, ref, s_ed.at[0], s_in.at[0], at(z, q, b)).wait_send()
 
             drains.append(drain)
-        earlier, drains[:] = list(drains), []
-        drain_now(earlier)
+        drain_now(settled)
 
         for m in range(J):
             arrive(rs_r.at[st, m, 2], r_rs.at[2 * (st * J + m) + 1])

time: 104 us -> 104 us (level)
  no operation moved by 1% of the time
where the time goes in v6:
time: 104 us
  Pallas kernels  101 us (97%)
  local copies, waits for them, and re-layouts  1.72 us (2%)
    pallas_call x1, Pallas kernels, per_device(): pl.pallas_call(functools.partial(kernel, dt), out_shape=jax.ShapeDtypeStr...  101 us

profile of v6, /device:TPU:1, one launch (start us, length us, event | category | flops | bytes accessed | tf_op | source)
XLA Modules:
  0.0 103.7 jit_solution(4447187425401397571)
XLA Ops:
  0.6 101.3 %shard_map.59 = bf16[4,3,32,384]{3,2,1,0:T(8,128)(2,1)} custom-call(bf16[2,3,32,384]{3,2,1,0:T(8,128)(2,1)} %bitcast.7, bf16[2,3,32,384]{3,2,1,0:T(8,128)(2,1)} %bitcast.8, bf16[32,32]{1,0:T(8,128)(2,1)} %hopping.1, f32[1,32]{1,0:T(1,128)} %bitcast.9), custom_call_target="tpu_custom_call" | custom-call | flops 4000000000 | bytes 1000000 | tf_op jit(solution)/shard_map/pallas_call | solution.py:475
  102.0 1.7 %fusion = (bf16[2,3,32,384]{3,2,1,0:T(8,128)(2,1)}, bf16[2,3,32,384]{3,2,1,0:T(8,128)(2,1)}) fusion(bf16[4,3,32,384]{3,2,1,0:T(8,128)(2,1)} %shard_map.59), kind=kLoop, calls=%fused_computation | loop fusion | bytes 589824 | tf_op jit(solution)/shard_map/slice | solution.py:487
